TPU v7x, 128 devices: a whole 4x4x4 slice. The times are simulated.
128 devices in a mesh: grp: 8 (over z, core), dev: 16 (over x, y).
Axes of the slice: x: 4, y: 4, z: 4, core: 2. Of those that a mesh axis runs over, the one named last changes fastest.
Arguments:
- velocity_old: float32 [512, 3, 32, 1024], P(('grp', 'dev')), may hold values from -6 to 6
- viscosity_old: float32 [512, 32, 1024], P(('grp', 'dev')), may hold values from 0.25 to 4
- source: int32 [512], replicated, may hold values from 0 to 511, as said below
Outputs:
- velocity_new: float32 [512, 3, 32, 1024], P(('grp', 'dev'))
Inputs may be any that keep to these rules, and one draw needn't show every extreme that they name: `source`: A permutation; the old block of new block b lies in the same agglomeration group and has the same place among its device's 4 blocks; the 4 blocks of a new device come from 4 different old devices of its group, and each old device sends 1 block to each of 4 different new devices.
All inputs are finite; a program needn't handle non-finite values.
Results may differ from a plain program's by a relative error of at most 0.0001.
Values sent between devices are 32-bit elements; how exact they have to be, the bound alone decides.
A program may use at most 256 MiB of HBM per device.

v0:
```python
import math

import jax
import jax.numpy as jnp
from jax import lax
from jax.sharding import PartitionSpec as P

SWEEPS = 2
BOTTOM = 8


RELAX_WEIGHT = 0.8
DIFFUSION_NUMBER = 1000.0


def padded_2(cells, sides, width):
    for axis, dim in sides:
        count = lax.axis_size(axis)
        ends = count - 1
        head = lax.slice_in_dim(cells, 0, width, axis=dim)
        tail = lax.slice_in_dim(cells, cells.shape[dim] - width, cells.shape[dim], axis=dim)
        cells = jnp.concatenate(
            [
                lax.ppermute(tail, axis, [(i, (i + 1) % count) for i in range(ends)]),
                cells,
                lax.ppermute(head, axis, [((i + 1) % count, i) for i in range(ends)]),
            ],
            axis=dim,
        )
    return cells


def blocks_to_grid(blocks):
    num_blocks, channels, edge_len = (blocks.shape[0], blocks.shape[1], blocks.shape[2])
    columns = num_blocks // 4
    parted = blocks.reshape(columns, 2, 2, channels, edge_len, edge_len, edge_len)
    parted = parted.transpose(3, 0, 6, 1, 4, 2, 5)
    return parted.reshape(channels, columns * edge_len, 4 * edge_len * edge_len)


def grid_to_blocks(grid):
    channels, length, plane = grid.shape
    edge_len = math.isqrt(plane) // 2
    columns = length // edge_len
    parted = grid.reshape(channels, columns, edge_len, 2, edge_len, 2, edge_len)
    parted = parted.transpose(1, 3, 5, 0, 4, 6, 2)
    return parted.reshape(columns * 4, channels, edge_len, edge_len * edge_len)


def flat_neighbors(array):
    plane = array.shape[2]
    width_y = math.isqrt(plane)
    middle = array[:, 1:-1]
    padded = jnp.pad(middle, ((0, 0), (0, 0), (width_y, width_y)))
    column = jnp.arange(plane) % width_y
    lower_y = jnp.where(column == 0, 0.0, padded[:, :, width_y - 1 : width_y - 1 + plane])
    upper_y = jnp.where(column == width_y - 1, 0.0, padded[:, :, width_y + 1 : width_y + 1 + plane])
    return (
        middle,
        (
            array[:, :-2],
            array[:, 2:],
            padded[:, :, 0:plane],
            padded[:, :, 2 * width_y : 2 * width_y + plane],
            lower_y,
            upper_y,
        ),
    )


def coefficients(viscous, level_coef, pad_along):
    middle, beside_all = flat_neighbors(pad_along(viscous))
    face_coef = tuple((0.5 * (middle + neighbor) for neighbor in beside_all))
    summed = face_coef[0] + face_coef[1] + face_coef[2] + face_coef[3] + face_coef[4] + face_coef[5]
    diagonal = 1.0 + level_coef * summed
    return (face_coef, diagonal)


def operate(solution, face_coef, diagonal, level_coef, pad_along):
    middle, beside_all = flat_neighbors(pad_along(solution))
    summed = face_coef[0] * beside_all[0]
    for index_no in range(1, 6):
        summed = summed + face_coef[index_no] * beside_all[index_no]
    return diagonal * solution - level_coef * summed


def smooth(solution, right_side, face_coef, diagonal, level_coef, pad_along, repeats):
    for sweep_no in range(repeats):
        solution = (
            solution
            + RELAX_WEIGHT
            * (right_side - operate(solution, face_coef, diagonal, level_coef, pad_along))
            / diagonal
        )
    return solution


def coarsen(grid):
    channels, length, plane = grid.shape
    width_y = math.isqrt(plane)
    shaped = grid.reshape(channels, length // 2, 2, width_y // 2, 2, width_y // 2, 2)
    return shaped.mean(axis=(2, 4, 6)).reshape(channels, length // 2, plane // 4)


def refine(grid):
    channels, length, plane = grid.shape
    width_y = math.isqrt(plane)
    shaped = grid.reshape(channels, length, 1, width_y, 1, width_y, 1)
    shaped = jnp.broadcast_to(shaped, (channels, length, 2, width_y, 2, width_y, 2))
    return shaped.reshape(channels, 2 * length, 4 * plane)


def cell_pad(array):
    return padded_2(array, ((("grp", "dev"), 1),), 1)


def group_pad(array):
    return padded_2(array, (("grp", 1),), 1)


def group_bottom(level_rhs, viscous):
    stacked = jnp.concatenate([level_rhs, viscous], axis=0)
    gathered = lax.all_gather(stacked, "dev", axis=1, tiled=True)
    group_rhs = gathered[:3]
    group_visc = gathered[3:]
    level_coef = DIFFUSION_NUMBER / 64.0
    face_coef, diagonal = coefficients(group_visc, level_coef, group_pad)
    solved = smooth(
        jnp.zeros_like(group_rhs), group_rhs, face_coef, diagonal, level_coef, group_pad, BOTTOM
    )
    own_width = level_rhs.shape[1]
    return lax.dynamic_slice_in_dim(solved, lax.axis_index("dev") * own_width, own_width, 1)


def vcycle_solve(right_side, viscous):
    stored = []
    solution = right_side
    level_rhs = right_side
    for level_no in range(3):
        level_coef = DIFFUSION_NUMBER / 4.0**level_no
        face_coef, diagonal = coefficients(viscous, level_coef, cell_pad)
        solution = smooth(solution, level_rhs, face_coef, diagonal, level_coef, cell_pad, SWEEPS)
        residue = level_rhs - operate(solution, face_coef, diagonal, level_coef, cell_pad)
        stored.append((solution, level_rhs, face_coef, diagonal, level_coef))
        level_rhs = coarsen(residue)
        viscous = coarsen(viscous)
        solution = jnp.zeros_like(level_rhs)
    solution = group_bottom(level_rhs, viscous)
    for level_no in (2, 1, 0):
        before, level_rhs, face_coef, diagonal, level_coef = stored[level_no]
        solution = smooth(
            before + refine(solution), level_rhs, face_coef, diagonal, level_coef, cell_pad, SWEEPS
        )
    return solution


def local(velocity_old, viscosity_old, source):
    group_index = lax.axis_index("grp")
    member_index = lax.axis_index("dev")
    member_count = lax.axis_size("dev")
    blk_per = velocity_old.shape[0]
    group_base = group_index * member_count * blk_per
    src_table = (
        lax.dynamic_slice_in_dim(source, group_base, member_count * blk_per).reshape(
            member_count, blk_per
        )
        - group_base
    )
    from_dev = src_table // blk_per
    from_slot = src_table % blk_per
    mine_dev = lax.dynamic_index_in_dim(from_dev, member_index, 0, keepdims=False)
    mine_slot = lax.dynamic_index_in_dim(from_slot, member_index, 0, keepdims=False)
    wanted = mine_dev * blk_per + mine_slot
    pieces = (
        lax.all_gather(velocity_old, "dev", axis=0, tiled=True),
        lax.all_gather(viscosity_old, "dev", axis=0, tiled=True),
    )
    piece_rows = pieces[0].shape[0]
    inside = (wanted >= 0) & (wanted < piece_rows)
    clipped = jnp.clip(wanted, 0, piece_rows - 1)
    new_vel = jnp.where(
        inside[:, None, None, None],
        jnp.take(pieces[0], clipped, axis=0),
        jnp.zeros_like(velocity_old),
    )
    new_visc = jnp.where(
        inside[:, None, None], jnp.take(pieces[1], clipped, axis=0), jnp.zeros_like(viscosity_old)
    )
    right_side = blocks_to_grid(new_vel)
    viscous = blocks_to_grid(new_visc[:, None])
    solution = vcycle_solve(right_side, viscous)
    return grid_to_blocks(solution)


def solution(mesh):
    return jax.shard_map(
        local,
        mesh=mesh,
        in_specs=(P(("grp", "dev"), None, None, None), P(("grp", "dev"), None, None), P()),
        out_specs=P(("grp", "dev"), None, None, None),
        check_vma=False,
    )
```

profile of v0, /device:TPU:0, one launch (start us, length us, event | category | flops | bytes accessed | tf_op | source)
XLA Modules:
  0.0 1002.4 jit_solution(10775965139218544529)
XLA Ops:
  18.6 64.0 %all-gather.5.cloned.1.call-done = f32[64,32,1024]{2,1,0:T(8,128)} async-done(((f32[4,32,1024]{2,1,0:T(8,128)}), f32[64,32,1024]{2,1,0:T(8,128)}) %all-gather.5.cloned.1.call-update) | async-done | bytes 8388624 | tf_op jit(solution)/shard_map/all_gather | solution.py:176
  89.0 22.0 %reshape_reshape.2 = f32[16,2,32,2,32,2]{1,0,5,4,3,2:T(8,128)} reshape(f32[1,1,32,2,32,2,32]{2,6,5,4,3,1,0:T(8,128)} %fusion.454) | data formatting | bytes 1048576 | tf_op jit(solution)/shard_map/reshape;reshape | solution.py:101
  111.0 12.6 %reduce_sum.55 = f32[16,32,32]{0,2,1:T(8,128)S(1)} reduce(f32[16,2,32,2,32,2]{1,0,5,4,3,2:T(8,128)} %reshape_reshape.2, f32[]{:T(128)} %constant.250.clone.1), dimensions={1,3,5}, to_apply=%region_1.2 | reduce | flops 114688 | bytes 589828 | tf_op jit(solution)/shard_map/reduce_sum | solution.py:102
  140.2 98.7 %all-gather.3.cloned.1.call-done = f32[64,3,32,1024]{3,2,1,0:T(8,128)} async-done(((f32[4,3,32,1024]{3,2,1,0:T(8,128)}), f32[64,3,32,1024]{3,2,1,0:T(8,128)}) %all-gather.3.cloned.1.call-update) | async-done | bytes 25165840 | tf_op jit(solution)/shard_map/all_gather | solution.py:175
  238.9 8.8 gather_fusion
  251.8 10.0 copy.71
  261.8 11.8 %select_bitcast_fusion = f32[3,1,32,2,32,2,32]{6,5,4,3,2,0,1:T(2,128)} fusion(f32[1,2,2,3,32,32,32]{5,2,4,1,6,3,0:T(2,128)} %copy.71, pred[2,2]{1,0:T(4,128)(4,1)S(1)} %compare_and_fusion, pred[2,2]{1,0:T(4,128)(4,1)S(1)} %and.182), kind=kLoop, calls=%fused_computation.2 | loop fusion | flops 786432 | bytes 3145736 | tf_op jit(solution)/shard_map/transpose | solution.py:37
  273.6 9.5 reshape.248
  320.0 7.2 collective-permute-start.10
  327.2 6.2 collective-permute-start.16
  336.5 154.0 %reshape.250 = f32[3,16,2,32,2,32,2]{6,5,4,3,2,1,0:T(8,128)} reshape(f32[3,32,4096]{2,1,0:T(8,128)} %fusion.35) | data formatting | bytes 3145728 | tf_op jit(solution)/shard_map/reshape | solution.py:101
  490.5 31.6 %reduce_sum.54 = f32[3,16,32,32]{3,2,1,0:T(8,128)} reduce(f32[3,16,2,32,2,32,2]{6,5,4,3,2,1,0:T(8,128)} %reshape.250, f32[]{:T(128)} %constant.250.clone.1), dimensions={2,4,6}, to_apply=%region_0.1 | reduce | flops 344064 | bytes 1769476 | tf_op jit(solution)/shard_map/reduce_sum | solution.py:102
  550.9 14.7 %reshape.251 = f32[3,8,2,16,2,16,2]{6,5,4,3,2,1,0:T(8,128)} reshape(f32[3,16,1024]{2,1,0:T(8,128)} %fusion.106) | data formatting | bytes 393216 | tf_op jit(solution)/shard_map/reshape | solution.py:101
  565.6 6.3 reduce_sum.56
  575.4 6.0 collective-permute-start.20
  584.6 13.2 %collective-permute-start.26 = (f32[3,1,64]{2,0,1:T(4,128)}, f32[3,1,64]{2,0,1:T(4,128)}, u32[]{:S(2)}, u32[]{:S(2)}) collective-permute-start(f32[3,1,64]{2,0,1:T(4,128)} %broadcast.453), channel_id=1, source_target_pairs={{0,16},{16,32},{32,48},{48,64},{64,80},{80,96},{96,112},{1,17},{17... | collective-permute-start | bytes 2312 | tf_op jit(solution)/shard_map/ppermute | solution.py:24
  611.5 34.7 %all_gather.11 = f32[4,64,64]{2,0,1:T(4,128)S(1)} all-gather(f32[4,4,64]{2,0,1:T(4,128)S(1)} %copy.76), channel_id=1, replica_groups=mesh['grp'=8,'dev'=16] {'dev'}, dimensions={1}, use_global_device_ids=true | all-gather | bytes 69632 | tf_op jit(solution)/shard_map/all_gather | solution.py:123
  730.9 5.8 broadcast_in_dim.360
  736.7 10.4 %reshape.254 = f32[3,16,1024]{2,1,0:T(8,128)} reshape(f32[3,8,2,16,2,16,2]{6,5,4,3,2,1,0:T(8,128)} %broadcast_in_dim.360) | data formatting | bytes 393216 | tf_op jit(solution)/shard_map/reshape | solution.py:110
  773.3 32.2 %broadcast_in_dim.362 = f32[3,16,2,32,2,32,2]{6,5,4,3,2,1,0:T(8,128)} broadcast(f32[3,16,32,32]{3,2,1,0:T(8,128)} %broadcast_in_dim.361), dimensions={0,1,3,5} | broadcast | bytes 1769472 | tf_op jit(solution)/shard_map/broadcast_in_dim | solution.py:109
  805.5 138.7 %reshape.255 = f32[3,32,4096]{2,1,0:T(8,128)} reshape(f32[3,16,2,32,2,32,2]{6,5,4,3,2,1,0:T(8,128)} %broadcast_in_dim.362) | data formatting | bytes 3145728 | tf_op jit(solution)/shard_map/reshape | solution.py:110
  971.6 7.7 reshape.256
  979.3 10.1 %copy.78 = f32[1,2,2,3,32,32,32]{6,5,4,3,2,1,0:T(8,128)} copy(f32[1,2,2,3,32,32,32]{5,2,4,1,6,3,0:T(2,128)} %bitcast.84) | data formatting | bytes 3145728 | tf_op jit(solution)/shard_map/transpose | solution.py:46
  989.4 5.9 reshape.257
  (351 shorter events, 264.8 us)
Async XLA Ops:
  6.5 76.1 %all-gather.5.cloned.1.call-start = ((), (), s32[]{:S(2)}) async-start(), calls=%async_computation.1 | async-start | bytes 8912896 | tf_op jit(solution)/shard_map/all_gather | solution.py:176
  7.3 231.7 %all-gather.3.cloned.1.call-start = ((), (), s32[]{:S(2)}) async-start(), calls=%async_computation | async-start | bytes 26738688 | tf_op jit(solution)/shard_map/all_gather | solution.py:175
  8.6 565.9 %collective-permute-start.19 = (f32[3,1,256]{2,1,0:T(1,128)}, f32[3,1,256]{2,1,0:T(1,128)}, u32[]{:S(2)}, u32[]{:S(2)}) collective-permute-start(f32[3,1,256]{2,1,0:T(1,128)} %broadcast.449), channel_id=1, source_target_pairs={{1,0},{2,1},{3,2},{4,3},{5,4},{6,5},{7,6},{8,7},{9,8},{10,9},{11,1... | collective-permute-start | bytes 9224 | tf_op jit(solution)/shard_map/ppermute | solution.py:26
  9.9 564.7 %collective-permute-start.18 = (f32[3,1,256]{2,1,0:T(1,128)}, f32[3,1,256]{2,1,0:T(1,128)}, u32[]{:S(2)}, u32[]{:S(2)}) collective-permute-start(f32[3,1,256]{2,1,0:T(1,128)} %broadcast.449), channel_id=1, source_target_pairs={{0,1},{1,2},{2,3},{3,4},{4,5},{5,6},{6,7},{7,8},{8,9},{9,10},{10,1... | collective-permute-start | bytes 9224 | tf_op jit(solution)/shard_map/ppermute | solution.py:24
  15.6 510.2 %collective-permute-start.11 = (f32[3,1,1024]{2,1,0:T(1,128)}, f32[3,1,1024]{2,1,0:T(1,128)}, u32[]{:S(2)}, u32[]{:S(2)}) collective-permute-start(f32[3,1,1024]{2,1,0:T(1,128)} %broadcast.445), channel_id=1, source_target_pairs={{1,0},{2,1},{3,2},{4,3},{5,4},{6,5},{7,6},{8,7},{9,8},{10,9},{11,1... | collective-permute-start | bytes 36872 | tf_op jit(solution)/shard_map/ppermute | solution.py:26
  131.7 151.5 %collective-permute-start = (f32[1,1,4096]{2,1,0:T(1,128)S(1)}, f32[1,1,4096]{2,1,0:T(1,128)S(1)}, u32[]{:S(2)}, u32[]{:S(2)}) collective-permute-start(f32[1,1,4096]{2,1,0:T(1,128)S(1)} %get-tuple-element.39), channel_id=1, source_target_pairs={{0,1},{1,2},{2,3},{3,4},{4,5},{5,6},{6,7},{7,8},{8,9},{9,10},{10,1... | collective-permute-start | bytes 49160 | tf_op jit(solution)/shard_map/ppermute | solution.py:24
  135.0 151.3 %collective-permute-start.1 = (f32[1,1,4096]{2,1,0:T(1,128)S(1)}, f32[1,1,4096]{2,1,0:T(1,128)S(1)}, u32[]{:S(2)}, u32[]{:S(2)}) collective-permute-start(f32[1,1,4096]{2,1,0:T(1,128)S(1)} %get-tuple-element.40), channel_id=1, source_target_pairs={{1,0},{2,1},{3,2},{4,3},{5,4},{6,5},{7,6},{8,7},{9,8},{10,9},{11,1... | collective-permute-start | bytes 49160 | tf_op jit(solution)/shard_map/ppermute | solution.py:26
  283.2 9.6 collective-permute-start.2
  286.2 11.1 %collective-permute-start.3 = (f32[3,1,4096]{2,1,0:T(1,128)S(1)}, f32[3,1,4096]{2,1,0:T(1,128)S(1)}, u32[]{:S(2)}, u32[]{:S(2)}) collective-permute-start(f32[3,1,4096]{2,1,0:T(1,128)S(1)} %get-tuple-element.31), channel_id=1, source_target_pairs={{1,0},{2,1},{3,2},{4,3},{5,4},{6,5},{7,6},{8,7},{9,8},{10,9},{11,1... | collective-permute-start | bytes 147464 | tf_op jit(solution)/shard_map/ppermute | solution.py:26
  292.8 7.9 collective-permute-start.8
  297.3 7.9 collective-permute-start.9
  300.7 6.6 collective-permute-start.4
  313.4 6.6 collective-permute-start.6
  317.9 9.3 collective-permute-start.7
  320.0 207.3 %collective-permute-start.10 = (f32[3,1,1024]{2,1,0:T(1,128)}, f32[3,1,1024]{2,1,0:T(1,128)}, u32[]{:S(2)}, u32[]{:S(2)}) collective-permute-start(f32[3,1,1024]{2,1,0:T(1,128)} %broadcast.445), channel_id=1, source_target_pairs={{0,1},{1,2},{2,3},{3,4},{4,5},{5,6},{6,7},{7,8},{8,9},{9,10},{10,1... | collective-permute-start | bytes 36872 | tf_op jit(solution)/shard_map/ppermute | solution.py:24
  327.2 206.0 %collective-permute-start.16 = (f32[1,1,256]{2,1,0:T(1,128)}, f32[1,1,256]{2,1,0:T(1,128)}, u32[]{:S(2)}, u32[]{:S(2)}) collective-permute-start(f32[1,1,256]{2,1,0:T(1,128)} %get-tuple-element.89), channel_id=1, source_target_pairs={{0,1},{1,2},{2,3},{3,4},{4,5},{5,6},{6,7},{7,8},{8,9},{9,10},{10,1... | collective-permute-start | bytes 3080 | tf_op jit(solution)/shard_map/ppermute | solution.py:24
  525.8 8.7 collective-permute-start.17
  528.6 7.3 collective-permute-start.12
  540.0 6.4 collective-permute-start.14
  575.4 24.6 %collective-permute-start.20 = (f32[3,1,256]{2,1,0:T(1,128)S(1)}, f32[3,1,256]{2,1,0:T(1,128)S(1)}, u32[]{:S(2)}, u32[]{:S(2)}) collective-permute-start(f32[3,1,256]{2,1,0:T(1,128)S(1)} %get-tuple-element.81), channel_id=1, source_target_pairs={{0,1},{1,2},{2,3},{3,4},{4,5},{5,6},{6,7},{7,8},{8,9},{9,10},{10,1... | collective-permute-start | bytes 9224 | tf_op jit(solution)/shard_map/ppermute | solution.py:24
  581.5 18.6 %collective-permute-start.21 = (f32[3,1,256]{2,1,0:T(1,128)S(1)}, f32[3,1,256]{2,1,0:T(1,128)S(1)}, u32[]{:S(2)}, u32[]{:S(2)}) collective-permute-start(f32[3,1,256]{2,1,0:T(1,128)S(1)} %get-tuple-element.82), channel_id=1, source_target_pairs={{1,0},{2,1},{3,2},{4,3},{5,4},{6,5},{7,6},{8,7},{9,8},{10,9},{11,1... | collective-permute-start | bytes 9224 | tf_op jit(solution)/shard_map/ppermute | solution.py:26
  583.4 69.4 %collective-permute-start.27 = (f32[3,1,64]{2,0,1:T(4,128)}, f32[3,1,64]{2,0,1:T(4,128)}, u32[]{:S(2)}, u32[]{:S(2)}) collective-permute-start(f32[3,1,64]{2,0,1:T(4,128)} %broadcast.453), channel_id=1, source_target_pairs={{16,0},{32,16},{48,32},{64,48},{80,64},{96,80},{112,96},{17,1},{33... | collective-permute-start | bytes 2312 | tf_op jit(solution)/shard_map/ppermute | solution.py:26
  584.6 68.1 %collective-permute-start.26 = (f32[3,1,64]{2,0,1:T(4,128)}, f32[3,1,64]{2,0,1:T(4,128)}, u32[]{:S(2)}, u32[]{:S(2)}) collective-permute-start(f32[3,1,64]{2,0,1:T(4,128)} %broadcast.453), channel_id=1, source_target_pairs={{0,16},{16,32},{32,48},{48,64},{64,80},{80,96},{96,112},{1,17},{17... | collective-permute-start | bytes 2312 | tf_op jit(solution)/shard_map/ppermute | solution.py:24
  748.2 6.9 collective-permute-start.46
  (97 other events, 4061.0 us)
Sparse Core Ops, SparseCore 0:
  9.5 73.0 all-gather.4
  84.8 154.0 all-gather.2
where the time goes:
time: 1020 us; the launch traced here: 1000 us
  local copies, waits for them, and re-layouts  462 us (45%)
  waiting for transfers between devices  219 us (21%)
  starting transfers between devices  155 us (15%)
  other arithmetic  115 us (11%)
  blocking collectives  34.7 us (3%)
  between operations  15.6 us (2%)
    reshape x3, local copies, waits for them, and re-layouts, coarsen(): grid.reshape(channels, length // 2, 2, width_y // 2, 2, width_y // 2, 2)  171 us
    reshape x3, local copies, waits for them, and re-layouts, refine(): return shaped.reshape(channels, 2 * length, 4 * plane)  151 us
    ppermute x27, starting transfers between devices, padded_2(): lax.ppermute(tail, axis, [(i, (i + 1) % count) for i in range(ends)])  119 us
    all_gather x1, waiting for transfers between devices, local(): lax.all_gather(velocity_old, 'dev', axis=0, tiled=True)  98.7 us
    all_gather x1, waiting for transfers between devices, local(): lax.all_gather(viscosity_old, 'dev', axis=0, tiled=True)  64 us
    reduce_sum x6, other arithmetic, coarsen(): shaped.mean(axis=(2, 4, 6)).reshape(channels, length // 2, plane // 4)  56.2 us
    ppermute x27, waiting for transfers between devices, padded_2(): lax.ppermute(head, axis, [((i + 1) % count, i) for i in range(ends)])  54.4 us
    broadcast_in_dim x6, local copies, waits for them, and re-layouts, refine(): jnp.broadcast_to(shaped, (channels, length, 2, width_y, 2, width_y, 2))  42.3 us
  transfers between devices with their start and end apart: 56, of which 23 were waited for; matrix products, arithmetic and copies ran while one was open for 34% of the time, Pallas kernels for 0%

commit v1 on v0

v1 whole, which is shorter than its diff:
```python
import jax
import jax.numpy as jnp
from jax import lax
from jax.experimental import pallas as pl
from jax.experimental.pallas import tpu as pltpu
from jax.sharding import PartitionSpec as P

F32 = jnp.float32
SIDE = 32
LANES = 128
DIFFUSION_NUMBER = 1000.0
RELAX = 0.8
BOTTOM = 8
LANE_SLOTS = (0, 2, 1, 3)
H0, H1, H2 = 4, 5, 6
N0, N1, N2, N3 = 32, 16, 8, 4
REACH = 3
H3 = REACH * N3
VMEM_LIMIT = 48 * 1024 * 1024
MESH = pl.DeviceIdType.MESH
HIGHEST = lax.Precision.HIGHEST


def positions():
    grp, dev = lax.axis_index("grp"), lax.axis_index("dev")
    n_grp, n_dev = lax.axis_size("grp"), lax.axis_size("dev")
    return grp, dev, n_grp, n_dev


def stream_device(offset):
    grp, dev, n_grp, n_dev = positions()
    at = lax.rem(grp * n_dev + dev + offset + n_grp * n_dev, n_grp * n_dev)
    return (at // n_dev, lax.rem(at, n_dev))


def multiple(value, of):
    return pl.multiple_of(value, of)


def regrid_kernel(
    source_ref, vel_ref, vis_ref, o_nu, o_0, o_1, o_2,
    st_0, st_1, st_2, st_3, mid_0, mid_1, mid_2, mid_3, as_0, as_1, as_2, as_3,
    send_1, recv_1, send_2, recv_2, send_h, recv_h,
):
    grp, dev, n_grp, n_dev = positions()
    each = SIDE // n_dev
    rows = each * SIDE
    outs = (o_nu, o_0, o_1, o_2)
    stages = (st_0, st_1, st_2, st_3)
    mids = (mid_0, mid_1, mid_2, mid_3)
    asms = (as_0, as_1, as_2, as_3)
    left, right = stream_device(-1), stream_device(1)

    barrier = pltpu.get_barrier_semaphore()

    def greet(t, carry):
        pl.semaphore_signal(
            barrier, inc=1, device_id=(grp, lax.rem(dev + t, n_dev)), device_id_type=MESH
        )
        return carry

    lax.fori_loop(1, n_dev, greet, 0)
    for beside in (left, right):
        pl.semaphore_signal(barrier, inc=1, device_id=beside, device_id_type=MESH)

    def transpose_field(f):
        def tile(t, carry):
            lanes = pl.ds(multiple(t * LANES, LANES), LANES)
            if f == 0:
                parts = [vis_ref[b, :, lanes] for b in LANE_SLOTS]
            else:
                parts = [vel_ref[b, f - 1, :, lanes] for b in LANE_SLOTS]
            turned = jnp.concatenate(parts, axis=0).T
            for jj in range(4):
                stages[f][pl.ds(4 * t + jj, SIDE, stride=SIDE), :] = turned[
                    SIDE * jj : SIDE * jj + SIDE
                ]
            return carry

        lax.fori_loop(0, 8, tile, 0)

    def spread(f):
        def send(t, carry):
            to = lax.rem(dev + t, n_dev)
            pltpu.make_async_remote_copy(
                src_ref=stages[f].at[pl.ds(multiple(to * rows, rows), rows)],
                dst_ref=mids[f].at[dev],
                send_sem=send_1.at[f],
                recv_sem=recv_1.at[f],
                device_id=(grp, to),
                device_id_type=MESH,
            ).start()
            return carry

        pltpu.make_async_copy(
            stages[f].at[pl.ds(multiple(dev * rows, rows), rows)], mids[f].at[dev], recv_1.at[f]
        ).start()
        lax.fori_loop(1, n_dev, send, 0)

    group_of_lane = lax.broadcasted_iota(jnp.int32, (rows, LANES), 1) // SIDE

    def collect(f):
        pltpu.make_async_copy(mids[f], mids[f], recv_1.at[f]).wait()

        def assemble(to):
            base = (grp * n_dev + to) * 4
            made = None
            for at, slot in enumerate(LANE_SLOTS):
                old = lax.rem(source_ref[base + slot] // 4, n_dev)
                piece = mids[f][old]
                made = piece if made is None else jnp.where(group_of_lane == at, piece, made)
            asms[f][to] = made.reshape(each, SIDE, LANES)

        def send(t, carry):
            to = lax.rem(dev + t, n_dev)
            assemble(to)
            pltpu.make_async_remote_copy(
                src_ref=asms[f].at[to],
                dst_ref=outs[f].at[pl.ds(H0 + dev * each, each)],
                send_sem=send_2.at[f],
                recv_sem=recv_2.at[f],
                device_id=(grp, to),
                device_id_type=MESH,
            ).start()
            return carry

        assemble(dev)
        pltpu.make_async_copy(
            asms[f].at[dev], outs[f].at[pl.ds(H0 + dev * each, each)], recv_2.at[f]
        ).start()
        lax.fori_loop(1, n_dev, send, 0)

    def halo_copy(f, side):
        src = outs[f].at[pl.ds(H0 if side == 0 else N0, H0)]
        dst = outs[f].at[pl.ds(H0 + N0 if side == 0 else 0, H0)]
        return pltpu.make_async_remote_copy(
            src_ref=src,
            dst_ref=dst,
            send_sem=send_h.at[f, side],
            recv_sem=recv_h.at[f, side],
            device_id=left if side == 0 else right,
            device_id_type=MESH,
        )

    transpose_field(0)
    pl.semaphore_wait(barrier, n_dev + 1)
    spread(0)
    for f in range(1, 4):
        transpose_field(f)
        spread(f)
    for f in range(4):
        collect(f)
    for f in range(4):
        own = outs[f].at[pl.ds(H0, N0)]
        pltpu.make_async_copy(own, own, recv_2.at[f]).wait()
        for side in (0, 1):
            halo_copy(f, side).start()
    at = grp * n_dev + dev
    for f in range(4):
        for side in (0, 1):
            halo_copy(f, side).wait()

        @pl.when(at == 0)
        def _():
            outs[f][pl.ds(0, H0)] = jnp.zeros((H0, SIDE, LANES), F32)

        @pl.when(at == n_grp * n_dev - 1)
        def _():
            outs[f][pl.ds(H0 + N0, H0)] = jnp.zeros((H0, SIDE, LANES), F32)

    for f in range(4):
        most = stages[f].at[pl.ds(0, (n_dev - 1) * rows)]
        pltpu.make_async_copy(most, most, send_1.at[f]).wait()
        most = asms[f].at[pl.ds(0, n_dev - 1)]
        pltpu.make_async_copy(most, most, send_2.at[f]).wait()


def regrid(n_dev, source, velocity_old, viscosity_old):
    each = SIDE // n_dev
    vmem = pl.BlockSpec(memory_space=pltpu.VMEM)
    extended = jax.ShapeDtypeStruct((N0 + 2 * H0, SIDE, LANES), F32)
    return pl.pallas_call(
        regrid_kernel,
        out_shape=[extended] * 4,
        in_specs=[pl.BlockSpec(memory_space=pltpu.SMEM), vmem, vmem],
        out_specs=[vmem] * 4,
        scratch_shapes=[pltpu.VMEM((SIDE * SIDE, LANES), F32)] * 4
        + [pltpu.VMEM((n_dev, each * SIDE, LANES), F32)] * 4
        + [pltpu.VMEM((n_dev, each, SIDE, LANES), F32)] * 4
        + [pltpu.SemaphoreType.DMA((4,))] * 4
        + [pltpu.SemaphoreType.DMA((4, 2))] * 2,
        compiler_params=pltpu.CompilerParams(
            collective_id=0, has_side_effects=True, vmem_limit_bytes=VMEM_LIMIT
        ),
        name="regrid",
    )(source, velocity_old, viscosity_old)


class Level:
    def __init__(self, rows, wide, d):
        self.rows, self.wide, self.d = rows, wide, d
        self.shape = (rows, LANES)
        row = lax.broadcasted_iota(jnp.int32, self.shape, 0)
        lane = lax.broadcasted_iota(jnp.int32, self.shape, 1)
        deep = lax.rem(lane, wide)
        far = LANES - wide
        self.ok_zm = deep >= d
        self.ok_zp = deep < wide - d
        self.ok_ym = (row >= d) | (lane >= wide)
        self.ok_yp = (row < rows - d) | (lane < far)
        edge = lax.broadcasted_iota(jnp.int32, (8, LANES), 0)
        self.edge_m = edge < d
        self.edge_p = edge >= 8 - d

    def beside(self, a):
        rows, wide, d = self.rows, self.wide, self.d
        zm = pltpu.roll(a, d, 1)
        zp = pltpu.roll(a, LANES - d, 1)
        ym = pltpu.roll(a, d, 0)
        yp = pltpu.roll(a, rows - d, 0)
        head = ym[:8]
        head = jnp.where(self.edge_m, pltpu.roll(head, wide, 1), head)
        tail = yp[rows - 8 :]
        tail = jnp.where(self.edge_p, pltpu.roll(tail, LANES - wide, 1), tail)
        if rows > 8:
            ym = jnp.concatenate([head, ym[8:]], axis=0)
            yp = jnp.concatenate([yp[: rows - 8], tail], axis=0)
        else:
            ym, yp = head, tail
        return zm, zp, ym, yp


def pair_sum(a, d):
    row = lax.broadcasted_iota(jnp.int32, a.shape, 0)
    lane = lax.broadcasted_iota(jnp.int32, a.shape, 1)
    first = lax.rem(row // d, 2) == 0
    a = a + jnp.where(first, pltpu.roll(a, a.shape[0] - d, 0), pltpu.roll(a, d, 0))
    first = lax.rem(lane // d, 2) == 0
    return a + jnp.where(first, pltpu.roll(a, LANES - d, 1), pltpu.roll(a, d, 1))


def weights(level, coef, lo, hi, nu_at, rhs_at, inside, g_ref, iw_ref, s_refs, also=None):
    def plane(n, carry):
        nu = nu_at(n)
        xm, xp = nu_at(n - 1), nu_at(n + 1)
        zm, zp, ym, yp = level.beside(nu)
        zm = jnp.where(level.ok_zm, zm, 0.0)
        zp = jnp.where(level.ok_zp, zp, 0.0)
        ym = jnp.where(level.ok_ym, ym, 0.0)
        yp = jnp.where(level.ok_yp, yp, 0.0)
        total = 6.0 * nu + ((xm + xp) + (zm + zp) + (ym + yp))
        diag = 1.0 + (0.5 * coef) * total
        w = RELAX / diag
        k = w * jnp.where(inside(n), 0.5 * coef, 0.0)
        g_ref[0, n] = k * (nu + xm)
        g_ref[1, n] = k * (nu + xp)
        g_ref[2, n] = jnp.where(level.ok_zm, k * (nu + zm), 0.0)
        g_ref[3, n] = jnp.where(level.ok_zp, k * (nu + zp), 0.0)
        g_ref[4, n] = jnp.where(level.ok_ym, k * (nu + ym), 0.0)
        g_ref[5, n] = jnp.where(level.ok_yp, k * (nu + yp), 0.0)
        iw_ref[n] = diag * (1.0 / RELAX)
        for c in range(3):
            s_refs[c][n] = w * rhs_at(c, n)
        return carry

    lax.fori_loop(lo, hi, plane, 0)


def gathered(level, g, src, n):
    zm, zp, ym, yp = level.beside(src[n])
    return (
        (g[0] * src[n - 1] + g[1] * src[n + 1])
        + (g[2] * zm + g[3] * zp)
        + (g[4] * ym + g[5] * yp)
    )


def sweep(level, lo, hi, g_ref, s_refs, srcs, dsts, shift=0):
    def plane(n, carry):
        g = [g_ref[i, n] for i in range(6)]
        for c in range(3):
            dsts[c][n - shift] = (1.0 - RELAX) * srcs[c][n] + (
                s_refs[c][n] + gathered(level, g, srcs[c], n)
            )
        return carry

    lax.fori_loop(lo, hi, plane, 0)


def residual(level, n, g_ref, iw_ref, s_refs, srcs):
    g = [g_ref[i, n] for i in range(6)]
    return [
        iw_ref[n] * ((s_refs[c][n] + gathered(level, g, srcs[c], n)) - RELAX * srcs[c][n])
        for c in range(3)
    ]


def vcycle_kernel(
    nu_0, r_0, r_1, r_2, o_0, o_1, o_2,
    g0, iw0, s0_0, s0_1, s0_2, a0_0, a0_1, a0_2, b0_0, b0_1, b0_2, tmp, half,
    x1, g1, iw1, s1_0, s1_1, s1_2, a1_0, a1_1, a1_2,
    x2, g2, iw2, s2_0, s2_1, s2_2, a2_0, a2_1, a2_2,
    x3, g3, iw3, s3_0, s3_1, s3_2, a3_0, a3_1, a3_2,
    pk2, pk3, send_1, recv_1, send_2, recv_2, send_3, recv_3,
):
    grp, dev, n_grp, n_dev = positions()
    at = grp * n_dev + dev
    count = n_grp * n_dev
    hops = [k for k in range(-REACH, REACH + 1) if k]

    barrier = pltpu.get_barrier_semaphore()
    for k in hops:
        pl.semaphore_signal(barrier, inc=1, device_id=stream_device(k), device_id_type=MESH)

    def inside_of(own, halo):
        def inside(n):
            cell = at * own + n - halo
            return (cell >= 0) & (cell < count * own)

        return inside

    in0, in1 = inside_of(N0, H0), inside_of(N1, H1)
    in2, in3 = inside_of(N2, H2), inside_of(N3, H3)
    rhs0 = (r_0, r_1, r_2)
    s0, a0, b0 = (s0_0, s0_1, s0_2), (a0_0, a0_1, a0_2), (b0_0, b0_1, b0_2)
    s1, a1 = (s1_0, s1_1, s1_2), (a1_0, a1_1, a1_2)
    s2, a2 = (s2_0, s2_1, s2_2), (a2_0, a2_1, a2_2)
    s3, a3 = (s3_0, s3_1, s3_2), (a3_0, a3_1, a3_2)

    fine = Level(SIDE, 2 * SIDE, 1)
    lane_f = lax.broadcasted_iota(jnp.int32, (LANES, LANES), 0)
    lane_c = lax.broadcasted_iota(jnp.int32, (LANES, LANES), 1)
    target = (lane_f // 64) * 64 + lax.rem(lane_f, 64) // 2
    down_m = [jnp.where(lane_c == target + 32 * jh, 0.5, 0.0).astype(F32) for jh in (0, 1)]
    target_t = (lane_c // 64) * 64 + lax.rem(lane_c, 64) // 2
    up_m = [jnp.where(lane_f == target_t + 32 * jh, 1.0, 0.0).astype(F32) for jh in (0, 1)]

    def rows_halved(f, m, total):
        tmp[f] = total
        pairs = 0.25 * (tmp[f, pl.ds(0, 16, stride=2), :] + tmp[f, pl.ds(1, 16, stride=2), :])
        half[f, 0, m] = pairs[:8]
        half[f, 1, m] = pairs[8:]

    def lanes_halved(f):
        made = None
        for jh in (0, 1):
            part = jnp.dot(
                half[f, jh, :N1].reshape(N1 * 8, LANES), down_m[jh],
                precision=HIGHEST, preferred_element_type=F32,
            )
            made = part if made is None else made + part
        x1[pl.ds(H1, N1), f] = made.reshape(N1, 8, LANES)

    weights(
        fine, DIFFUSION_NUMBER, 1, N0 + 2 * H0 - 1, lambda n: nu_0[n], lambda c, n: rhs0[c][n],
        in0, g0, iw0, s0,
    )

    def nu_pairs(m, carry):
        rows_halved(3, m, nu_0[H0 + 2 * m] + nu_0[H0 + 2 * m + 1])
        return carry

    lax.fori_loop(0, N1, nu_pairs, 0)
    lanes_halved(3)
    sweep(fine, 1, N0 + 2 * H0 - 1, g0, s0, rhs0, a0)
    sweep(fine, 2, N0 + 2 * H0 - 2, g0, s0, a0, b0)

    def down_0(m, carry):
        n = H0 + 2 * m
        first = residual(fine, n, g0, iw0, s0, b0)
        second = residual(fine, n + 1, g0, iw0, s0, b0)
        for c in range(3):
            rows_halved(c, m, first[c] + second[c])
        return carry

    lax.fori_loop(0, N1, down_0, 0)
    for c in range(3):
        lanes_halved(c)

    pl.semaphore_wait(barrier, len(hops))

    def exchange(k, src, dst, send, recv):
        return pltpu.make_async_remote_copy(
            src_ref=src, dst_ref=dst, send_sem=send, recv_sem=recv,
            device_id=stream_device(k), device_id_type=MESH,
        )

    def blank(x, inside, ranges):
        for lo, hi in ranges:
            def plane(n, carry):
                x[n] = jnp.where(inside(n), x[n], 0.0)
                return carry

            lax.fori_loop(lo, hi, plane, 0)

    copies = [
        exchange(-1, x1.at[pl.ds(H1, H1)], x1.at[pl.ds(H1 + N1, H1)], send_1.at[0], recv_1.at[0]),
        exchange(1, x1.at[pl.ds(N1, H1)], x1.at[pl.ds(0, H1)], send_1.at[1], recv_1.at[1]),
    ]
    for copy in copies:
        copy.start()
    for copy in copies:
        copy.wait()
    blank(x1, in1, [(0, H1), (H1 + N1, N1 + 2 * H1)])
    lev1, lev2, lev3 = Level(8, SIDE, 1), Level(8, SIDE, 2), Level(8, SIDE, 4)
    weights(
        lev1, DIFFUSION_NUMBER / 4, 1, N1 + 2 * H1 - 1, lambda n: x1[n, 3], lambda c, n: x1[n, c],
        in1, g1, iw1, s1,
    )
    sweep(lev1, 2, N1 + 2 * H1 - 2, g1, s1, s1, a1)

    def down_1(m, carry):
        n = H1 + 2 * m
        first = residual(lev1, n, g1, iw1, s1, a1)
        second = residual(lev1, n + 1, g1, iw1, s1, a1)
        for c in range(3):
            x2[H2 + m, c] = 0.125 * pair_sum(first[c] + second[c], 1)
        x2[H2 + m, 3] = 0.125 * pair_sum(x1[n, 3] + x1[n + 1, 3], 1)
        return carry

    lax.fori_loop(0, N2, down_1, 0)

    row8 = lax.broadcasted_iota(jnp.int32, (8, LANES), 0)
    lane8 = lax.broadcasted_iota(jnp.int32, (8, LANES), 1)
    place2 = lax.rem(row8, 2) * 2 + lax.rem(lane8, 2)
    place3 = lax.rem(row8, 4) * 4 + lax.rem(lane8, 4)

    def pack_2(m, carry):
        made = x2[H2 + m, 0]
        for f in range(1, 4):
            made = jnp.where(place2 == f, x2[H2 + m, f], made)
        pk2[H2 + m] = made
        return carry

    lax.fori_loop(0, N2, pack_2, 0)
    copies = [
        exchange(-1, pk2.at[pl.ds(H2, H2)], pk2.at[pl.ds(H2 + N2, H2)], send_2.at[0], recv_2.at[0]),
        exchange(1, pk2.at[pl.ds(N2, H2)], pk2.at[pl.ds(0, H2)], send_2.at[1], recv_2.at[1]),
    ]
    for copy in copies:
        copy.start()
    for copy in copies:
        copy.wait()

    def unpack_2(n, carry):
        packed = jnp.where(in2(n), pk2[n], 0.0)
        for f in range(4):
            x2[n, f] = pair_sum(jnp.where(place2 == f, packed, 0.0), 1)
        return carry

    lax.fori_loop(0, H2, unpack_2, 0)
    lax.fori_loop(H2 + N2, N2 + 2 * H2, unpack_2, 0)
    weights(
        lev2, DIFFUSION_NUMBER / 16, 1, N2 + 2 * H2 - 1, lambda n: x2[n, 3], lambda c, n: x2[n, c],
        in2, g2, iw2, s2,
    )
    sweep(lev2, 2, N2 + 2 * H2 - 2, g2, s2, s2, a2)

    def down_2(m, carry):
        n = H2 + 2 * m
        first = residual(lev2, n, g2, iw2, s2, a2)
        second = residual(lev2, n + 1, g2, iw2, s2, a2)
        for c in range(3):
            x3[H3 + m, c] = 0.125 * pair_sum(first[c] + second[c], 2)
        x3[H3 + m, 3] = 0.125 * pair_sum(x2[n, 3] + x2[n + 1, 3], 2)
        return carry

    lax.fori_loop(0, N3, down_2, 0)

    made = x3[H3, 0]
    for m in range(N3):
        for f in range(4):
            if m or f:
                made = jnp.where(place3 == 4 * m + f, x3[H3 + m, f], made)
    pk3[REACH] = made
    copies = [
        exchange(k, pk3.at[REACH], pk3.at[REACH - k], send_3.at[i], recv_3.at[i])
        for i, k in enumerate(hops)
    ]
    for copy in copies:
        copy.start()
    for copy in copies:
        copy.wait()

    def unpack_3(b, carry):
        packed = pk3[b]
        for m in range(N3):
            n = N3 * b + m
            for f in range(4):
                one = jnp.where((place3 == 4 * m + f) & in3(n), packed, 0.0)
                x3[n, f] = pair_sum(pair_sum(one, 1), 2)
        return carry

    lax.fori_loop(0, REACH, unpack_3, 0)
    lax.fori_loop(REACH + 1, 2 * REACH + 1, unpack_3, 0)
    planes3 = N3 + 2 * H3
    lo = H3 - 2 - (BOTTOM - 1)
    weights(
        lev3, DIFFUSION_NUMBER / 64, lo, planes3 - lo, lambda n: x3[n, 3], lambda c, n: x3[n, c],
        in3, g3, iw3, s3,
    )
    b3 = [x3.at[:, c] for c in range(3)]
    src = s3
    for turn in range(1, BOTTOM):
        dst = a3 if turn % 2 else b3
        sweep(lev3, lo + turn, planes3 - lo - turn, g3, s3, src, dst)
        src = dst
    b2 = [x2.at[:, c] for c in range(3)]

    def add_3(n, carry):
        m = H3 - 2 + (n - (H2 - 4)) // 2
        for c in range(3):
            a2[c][n] = a2[c][n] + src[c][m]
        return carry

    lax.fori_loop(2, N2 + 2 * H2 - 2, add_3, 0)
    sweep(lev2, 3, N2 + 2 * H2 - 3, g2, s2, a2, b2)
    sweep(lev2, 4, N2 + 2 * H2 - 4, g2, s2, b2, a2)
    b1 = [x1.at[:, c] for c in range(3)]

    def add_2(n, carry):
        m = H2 - 2 + (n - (H1 - 4)) // 2
        for c in range(3):
            a1[c][n] = a1[c][n] + a2[c][m]
        return carry

    lax.fori_loop(2, N1 + 2 * H1 - 2, add_2, 0)
    sweep(lev1, 3, N1 + 2 * H1 - 3, g1, s1, a1, b1)
    sweep(lev1, 4, N1 + 2 * H1 - 4, g1, s1, b1, a1)
    wide = N1 + 2
    for c in range(3):
        coarse = a1[c][pl.ds(H1 - 1, wide)].reshape(wide * 8, LANES)
        for jh in (0, 1):
            half[c, jh] = jnp.dot(
                coarse, up_m[jh], precision=HIGHEST, preferred_element_type=F32
            ).reshape(wide, 8, LANES)

    def add_1(m, carry):
        for c in range(3):
            for jh in (0, 1):
                for twin in (0, 1):
                    tmp[c, pl.ds(16 * jh + twin, 8, stride=2), :] = half[c, jh, m]
            for twin in (0, 1):
                n = H0 - 2 + 2 * m + twin
                b0[c][n] = b0[c][n] + tmp[c]
        return carry

    lax.fori_loop(0, wide, add_1, 0)
    sweep(fine, 3, N0 + 2 * H0 - 3, g0, s0, b0, a0)
    sweep(fine, 4, N0 + 2 * H0 - 4, g0, s0, a0, (o_0, o_1, o_2), shift=H0)


def vcycle(fields):
    vmem = pl.BlockSpec(memory_space=pltpu.VMEM)

    def level_scratch(planes, rows, copies):
        one = pltpu.VMEM((planes, rows, LANES), F32)
        return [pltpu.VMEM((6, planes, rows, LANES), F32), one] + [one] * (3 * copies)

    n0, n1, n2, n3 = N0 + 2 * H0, N1 + 2 * H1, N2 + 2 * H2, N3 + 2 * H3
    return pl.pallas_call(
        vcycle_kernel,
        out_shape=[jax.ShapeDtypeStruct((N0, SIDE, LANES), F32)] * 3,
        in_specs=[vmem] * 4,
        out_specs=[vmem] * 3,
        scratch_shapes=level_scratch(n0, SIDE, 3)
        + [pltpu.VMEM((4, SIDE, LANES), F32), pltpu.VMEM((4, 2, N1 + 2, 8, LANES), F32)]
        + [pltpu.VMEM((n1, 4, 8, LANES), F32)] + level_scratch(n1, 8, 2)
        + [pltpu.VMEM((n2, 4, 8, LANES), F32)] + level_scratch(n2, 8, 2)
        + [pltpu.VMEM((n3, 4, 8, LANES), F32)] + level_scratch(n3, 8, 2)
        + [pltpu.VMEM((n2, 8, LANES), F32), pltpu.VMEM((2 * REACH + 1, 8, LANES), F32)]
        + [pltpu.SemaphoreType.DMA((2,))] * 4
        + [pltpu.SemaphoreType.DMA((2 * REACH,))] * 2,
        compiler_params=pltpu.CompilerParams(
            collective_id=1, has_side_effects=True, vmem_limit_bytes=VMEM_LIMIT
        ),
        name="vcycle",
    )(*fields)


def blocks_kernel(e_0, e_1, e_2, out_ref):
    for c, e in enumerate((e_0, e_1, e_2)):
        def tile(t, carry):
            parts = [e[pl.ds(4 * t + jj, SIDE, stride=SIDE), :] for jj in range(4)]
            turned = jnp.concatenate(parts, axis=0).T
            lanes = pl.ds(multiple(t * LANES, LANES), LANES)
            for at, slot in enumerate(LANE_SLOTS):
                out_ref[slot, c, :, lanes] = turned[SIDE * at : SIDE * at + SIDE]
            return carry

        lax.fori_loop(0, 8, tile, 0)


def to_blocks(planes):
    vmem = pl.BlockSpec(memory_space=pltpu.VMEM)
    return pl.pallas_call(
        blocks_kernel,
        out_shape=jax.ShapeDtypeStruct((4, 3, SIDE, SIDE * SIDE), F32),
        in_specs=[vmem] * 3,
        out_specs=vmem,
        compiler_params=pltpu.CompilerParams(vmem_limit_bytes=VMEM_LIMIT),
        name="to_blocks",
    )(*[p.reshape(SIDE * SIDE, LANES) for p in planes])


def solution(mesh):
    n_dev = mesh.shape["dev"]

    def local(velocity_old, viscosity_old, source):
        fields = regrid(n_dev, source, velocity_old, viscosity_old)
        return to_blocks(vcycle(fields))

    return jax.shard_map(
        local,
        mesh=mesh,
        in_specs=(P(("grp", "dev"), None, None, None), P(("grp", "dev"), None, None), P()),
        out_specs=P(("grp", "dev"), None, None, None),
        check_vma=False,
    )
```

time: 1020 us -> 135 us (0.13); the launches traced: 1000 us -> 135 us
  local copies, waits for them, and re-layouts: 462 us -> 3.13 us
  waiting for transfers between devices: 219 us -> 0 us
  starting transfers between devices: 155 us -> 0 us
  Pallas kernels: 0 us -> 132 us
  other arithmetic: 115 us -> 0 us
  blocking collectives: 34.7 us -> 0 us
  between operations: 15.6 us -> 0.02 us
    reshape x10 -> x0, local copies, waits for them, and re-layouts: 348 us -> none  [the longest x3 171 us: coarsen(): grid.reshape(channels, length // 2, 2, width_y // 2, 2, width_y // 2, 2)]
    all_gather x2 -> x0, waiting for transfers between devices: 163 us -> none  [the longest x1 98.7 us: local(): lax.all_gather(velocity_old, 'dev', axis=0, tiled=True)]
    ppermute x54 -> x0, starting transfers between devices: 155 us -> none  [the longest x27 119 us: padded_2(): lax.ppermute(tail, axis, [(i, (i + 1) % count) for i in range(ends)])]
    pallas_call x0 -> x3, Pallas kernels: none -> 132 us  [the longest x1 65.2 us: vcycle(): pl.pallas_call(vcycle_kernel, out_shape=[jax.ShapeDtypeStruct((N0, SIDE,...]
    reduce_sum x6 -> x0, other arithmetic: 56.2 us -> none  [coarsen(): shaped.mean(axis=(2, 4, 6)).reshape(channels, length // 2, plane // 4)]
    ppermute x54 -> x0, waiting for transfers between devices: 55.2 us -> none  [the longest x27 54.4 us: padded_2(): lax.ppermute(head, axis, [((i + 1) % count, i) for i in range(ends)])]
    broadcast_in_dim x9 -> x0, local copies, waits for them, and re-layouts: 42.3 us -> none  [the longest x6 42.3 us: refine(): jnp.broadcast_to(shaped, (channels, length, 2, width_y, 2, width_y, 2))]
    all_gather x1 -> x0, blocking collectives: 34.7 us -> none  [group_bottom(): gathered = lax.all_gather(stacked, 'dev', axis=1, tiled=True)]
  transfers between devices with their start and end apart: 56 -> 0, of which waited for: 23 -> 0; matrix products, arithmetic and copies ran while one was open for 34% -> 0% of each run, Pallas kernels for 0% -> 0%
where the time goes in v1:
time: 135 us
  Pallas kernels  132 us (98%)
  local copies, waits for them, and re-layouts  3.13 us (2%)
    pallas_call x1, Pallas kernels, vcycle(): pl.pallas_call(vcycle_kernel, out_shape=[jax.ShapeDtypeStruct((N0, SIDE,...  65.2 us
    pallas_call x1, Pallas kernels, regrid(): pl.pallas_call(regrid_kernel, out_shape=[extended] * 4, in_specs=[pl.Bloc...  63 us
    pallas_call x1, Pallas kernels, to_blocks(): pl.pallas_call(blocks_kernel, out_shape=jax.ShapeDtypeStruct((4, 3, SIDE,...  3.84 us
    unnamed x6, local copies, waits for them, and re-layouts  3.13 us

profile of v1, /device:TPU:0, one launch (start us, length us, event | category | flops | bytes accessed | tf_op | source)
XLA Modules:
  0.0 135.2 jit_solution(13695556322866957656)
XLA Ops:
  0.0 0.0 copy-start
  0.0 1.4 %copy-done = f32[4,3,32,1024]{3,2,1,0:T(8,128)S(1)} copy-done((f32[4,3,32,1024]{3,2,1,0:T(8,128)S(1)}, f32[4,3,32,1024]{3,2,1,0:T(8,128)}, u32[]{:S(2)}) %copy-start) | copy-done | bytes 1572888
  1.4 0.0 copy-start.1
  1.4 1.0 copy-done.1
  2.5 0.0 copy-start.2
  2.5 0.7 copy-done.2
  3.1 63.0 %regrid.1 = (f32[40,32,128]{2,1,0:T(8,128)S(1)}, f32[40,32,128]{2,1,0:T(8,128)S(1)}, f32[40,32,128]{2,1,0:T(8,128)S(1)}, f32[40,32,128]{2,1,0:T(8,128)S(1)}) custom-call(s32[512]{0:T(512)S(1)} %copy-done.2, f32[4,3,32,1024]{3,2,1,0:T(8,128)S(1)} %copy-done, f32[4,32,1024]{2,1,0:T(8,128)S(1)} %copy-done.1), custom_call_target="tpu_custom_call" | custom-call | tf_op jit(solution)/shard_map/regrid/pallas_call | solution.py:182
  66.1 65.2 %vcycle.1 = (f32[32,32,128]{2,1,0:T(8,128)S(1)}, f32[32,32,128]{2,1,0:T(8,128)S(1)}, f32[32,32,128]{2,1,0:T(8,128)S(1)}) custom-call(f32[40,32,128]{2,1,0:T(8,128)S(1)} %get-tuple-element.12.nu_0, f32[40,32,128]{2,1,0:T(8,128)S(1)} %get-tuple-element.13.r_0, f32[40,32,128]{2,1,0:T(8,128)S(1)} %get-tuple-element.14.r_1, f32[40,32,128]{2,1,0:T(8,128)S(1)} %get-tuple-element.15.r_2), custom_call_target="tpu_custom_call" | custom-call | tf_op jit(solution)/shard_map/vcycle/pallas_call | solution.py:561
  131.3 3.8 %to_blocks.1 = f32[4,3,32,1024]{3,2,1,0:T(8,128)} custom-call(f32[1024,128]{1,0:T(8,128)S(1)} %bitcast.3, f32[1024,128]{1,0:T(8,128)S(1)} %bitcast.4, f32[1024,128]{1,0:T(8,128)S(1)} %bitcast.5), custom_call_target="tpu_custom_call" | custom-call | tf_op jit(solution)/shard_map/to_blocks/pallas_call | solution.py:596
Async XLA Ops:
  0.0 1.4 %copy-start = (f32[4,3,32,1024]{3,2,1,0:T(8,128)S(1)}, f32[4,3,32,1024]{3,2,1,0:T(8,128)}, u32[]{:S(2)}) copy-start(f32[4,3,32,1024]{3,2,1,0:T(8,128)} %vel_ref.1) | copy-start | bytes 4718596
  1.4 1.0 copy-start.1
  2.5 0.7 copy-start.2

commit v2 on v0

v2 whole, which is shorter than its diff:
```python
import functools

import jax
import jax.numpy as jnp
from jax import lax
from jax.experimental import pallas as pl
from jax.experimental.pallas import tpu as pltpu
from jax.sharding import PartitionSpec as P

F32 = jnp.float32
SIDE = 32
LANES = 128
DIFFUSION_NUMBER = 1000.0
RELAX = 0.8
BOTTOM = 8
LANE_SLOTS = (0, 2, 1, 3)
H0, H1, H2 = 4, 5, 6
N0, N1, N2, N3 = 32, 16, 8, 4
REACH = 3
H3 = REACH * N3
VMEM_LIMIT = 48 * 1024 * 1024
MESH = pl.DeviceIdType.MESH
HIGHEST = lax.Precision.HIGHEST


def positions():
    grp, dev = lax.axis_index("grp"), lax.axis_index("dev")
    n_grp, n_dev = lax.axis_size("grp"), lax.axis_size("dev")
    return grp, dev, n_grp, n_dev


def stream_device(offset):
    grp, dev, n_grp, n_dev = positions()
    at = lax.rem(grp * n_dev + dev + offset + n_grp * n_dev, n_grp * n_dev)
    return (at // n_dev, lax.rem(at, n_dev))


TOP = 8
TALL = SIDE + 2 * TOP
BODY = slice(TOP, TOP + SIDE)


def multiple(value, of):
    return pl.multiple_of(value, of)


def put(ref, n, v):
    ref[n, BODY] = v
    ref[n, :TOP] = pltpu.roll(v[SIDE - TOP :], LANES // 2, 1)
    ref[n, TOP + SIDE :] = pltpu.roll(v[:TOP], LANES // 2, 1)


def fine_beside(ref, n, v):
    return (
        pltpu.roll(v, 1, 1),
        pltpu.roll(v, LANES - 1, 1),
        ref[n, TOP - 1 : TOP + SIDE - 1],
        ref[n, TOP + 1 : TOP + SIDE + 1],
    )


def steps(lo, hi, most, body):
    size = max(t for t in range(1, most + 1) if (hi - lo) % t == 0)

    def step(i, carry):
        body([lo + size * i + t for t in range(size)])
        return carry

    if size == hi - lo:
        step(0, 0)
    else:
        lax.fori_loop(0, (hi - lo) // size, step, 0)


class Level:
    def __init__(self, rows, wide, high, d):
        self.wide, self.d = wide, d
        row = lax.broadcasted_iota(jnp.int32, (rows, LANES), 0)
        lane = lax.broadcasted_iota(jnp.int32, (rows, LANES), 1)
        deep = lax.rem(lane, high)
        self.ok_zm = deep >= d
        self.ok_zp = deep < high - d
        self.ok_ym = (row >= d) | (lane >= wide)
        self.ok_yp = (row < rows - d) | (lane < LANES - wide)
        self.wrap_m = row < d
        self.wrap_p = row >= rows - d

    def beside(self, ref, n, a):
        wide, d = self.wide, self.d
        zm = pltpu.roll(a, d, 1)
        zp = pltpu.roll(a, LANES - d, 1)
        ym = pltpu.roll(a, d, 0)
        ym = jnp.where(self.wrap_m, pltpu.roll(ym, wide, 1), ym)
        yp = pltpu.roll(a, 8 - d, 0)
        yp = jnp.where(self.wrap_p, pltpu.roll(yp, LANES - wide, 1), yp)
        return zm, zp, ym, yp


class Fine(Level):
    def beside(self, ref, n, a):
        return fine_beside(ref, n, a)


def spread_rows(a, d):
    row = lax.broadcasted_iota(jnp.int32, a.shape, 0)
    first = lax.rem(row // d, 2) == 0
    return a + jnp.where(first, pltpu.roll(a, a.shape[0] - d, 0), pltpu.roll(a, d, 0))


def spread_lanes(a, d):
    lane = lax.broadcasted_iota(jnp.int32, a.shape, 1)
    first = lax.rem(lane // d, 2) == 0
    return a + jnp.where(first, pltpu.roll(a, LANES - d, 1), pltpu.roll(a, d, 1))


def pair_sum(a, d):
    return spread_lanes(spread_rows(a, d), d)


def weights(level, coef, lo, hi, most, nu_ref, at, inside, g_ref, w_ref, iw_ref):
    def planes(ns):
        made = []
        for n in ns:
            nu = nu_ref[n, at]
            xm, xp = nu_ref[n - 1, at], nu_ref[n + 1, at]
            zm, zp, ym, yp = level.beside(nu_ref, n, nu)
            zm = jnp.where(level.ok_zm, zm, 0.0)
            zp = jnp.where(level.ok_zp, zp, 0.0)
            ym = jnp.where(level.ok_ym, ym, 0.0)
            yp = jnp.where(level.ok_yp, yp, 0.0)
            total = 6.0 * nu + ((xm + xp) + (zm + zp) + (ym + yp))
            diag = 1.0 + (0.5 * coef) * total
            w = RELAX / diag
            k = w * jnp.where(inside(n), 0.5 * coef, 0.0)
            made.append(
                (
                    n, w, diag * (1.0 / RELAX), k * (nu + xm), k * (nu + xp),
                    jnp.where(level.ok_zm, k * (nu + zm), 0.0),
                    jnp.where(level.ok_zp, k * (nu + zp), 0.0),
                    jnp.where(level.ok_ym, k * (nu + ym), 0.0),
                    jnp.where(level.ok_yp, k * (nu + yp), 0.0),
                )
            )
        for n, w, iw, *g in made:
            w_ref[n] = w
            iw_ref[n] = iw
            for i in range(6):
                g_ref[i, n] = g[i]

    steps(lo, hi, most, planes)


def gathered(level, g, src, at, n, v):
    zm, zp, ym, yp = level.beside(src, n, v)
    return (
        (g[0] * src[n - 1, at] + g[1] * src[n + 1, at])
        + (g[2] * zm + g[3] * zp)
        + (g[4] * ym + g[5] * yp)
    )


ALL = slice(None)


def sweep(level, lo, hi, most, g_ref, s_refs, srcs, store, at=ALL):
    def planes(ns):
        made = []
        for n in ns:
            g = [g_ref[i, n] for i in range(6)]
            for c, (s, src) in enumerate(zip(s_refs, srcs)):
                v = src[n, at]
                made.append(
                    (c, n, (1.0 - RELAX) * v + (s[n] + gathered(level, g, src, at, n, v)))
                )
        for c, n, v in made:
            store(c, n, v)

    steps(lo, hi, most, planes)


def storing(refs):
    def store(c, n, v):
        refs[c][n] = v

    return store


def residual(level, n, g_ref, iw_ref, s_refs, srcs, at=ALL):
    g = [g_ref[i, n] for i in range(6)]
    made = []
    for s, src in zip(s_refs, srcs):
        v = src[n, at]
        made.append(iw_ref[n] * ((s[n] + gathered(level, g, src, at, n, v)) - RELAX * v))
    return made


def names_of_scratch(n_dev):
    each = SIDE // n_dev
    n0, n1, n2, n3 = N0 + 2 * H0, N1 + 2 * H1, N2 + 2 * H2, N3 + 2 * H3

    def vmem(*shape):
        return pltpu.VMEM((*shape, LANES), F32)

    def dma(*shape):
        return pltpu.SemaphoreType.DMA(shape)

    named = {"vis": pltpu.VMEM((4, SIDE, SIDE * SIDE), F32)}
    for c in range(3):
        named[f"vel{c}"] = pltpu.VMEM((4, SIDE, SIDE * SIDE), F32)
    for f in range(4):
        named[f"stage{f}"] = vmem(SIDE * SIDE)
        named[f"mid{f}"] = vmem(n_dev, each * SIDE)
        named[f"asm{f}"] = vmem(n_dev, each, SIDE)
        named[f"grid{f}"] = vmem(n0, TALL)
    named |= {"g0": vmem(6, n0, SIDE), "w0": vmem(n0, SIDE), "iw0": vmem(n0, SIDE)}
    for c in range(3):
        named[f"s0{c}"] = vmem(n0, SIDE)
        named[f"a0{c}"] = vmem(n0, TALL)
        named[f"b0{c}"] = vmem(n0, TALL)
    named |= {"tmp": vmem(3 * 3, SIDE), "half": vmem(4, 2, N1 + 2, 8)}
    for level, n in ((1, n1), (2, n2), (3, n3)):
        named |= {
            f"nu{level}": vmem(n, 8), f"x{level}": vmem(n, 3, 8), f"g{level}": vmem(6, n, 8),
            f"w{level}": vmem(n, 8), f"iw{level}": vmem(n, 8),
        }
        for c in range(3):
            for kind in "sab":
                named[f"{kind}{level}{c}"] = vmem(n, 8)
    named |= {
        "pk2": vmem(n2, 8), "pk3": vmem(2 * REACH + 1, 8), "in_sem": dma(4),
        "send_1": dma(4), "recv_1": dma(4), "send_2": dma(4), "recv_2": dma(4),
        "send_h": dma(4, 2), "recv_h": dma(4, 2), "send_e": dma(5, 2), "recv_e": dma(5, 2),
        "send_n3": dma(2 * REACH), "recv_n3": dma(2 * REACH),
        "send_r3": dma(2 * REACH), "recv_r3": dma(2 * REACH),
    }
    return named


def whole_kernel(names, source_ref, vel_hbm, vis_hbm, o_0, o_1, o_2, *scratch):
    r = dict(zip(names, scratch))
    grp, dev, n_grp, n_dev = positions()
    at = grp * n_dev + dev
    count = n_grp * n_dev
    each = SIDE // n_dev
    rows = each * SIDE
    hops = [k for k in range(-REACH, REACH + 1) if k]
    stages, mids = [r[f"stage{f}"] for f in range(4)], [r[f"mid{f}"] for f in range(4)]
    asms, grids = [r[f"asm{f}"] for f in range(4)], [r[f"grid{f}"] for f in range(4)]
    inputs = [r["vis"]] + [r[f"vel{c}"] for c in range(3)]

    def three(kind, level):
        return [r[f"{kind}{level}{c}"] for c in range(3)]

    loads = [pltpu.make_async_copy(vis_hbm, inputs[0], r["in_sem"].at[0])]
    loads += [
        pltpu.make_async_copy(vel_hbm.at[:, c], inputs[1 + c], r["in_sem"].at[1 + c])
        for c in range(3)
    ]
    for load in loads:
        load.start()
    barrier = pltpu.get_barrier_semaphore()

    def greet(t, carry):
        pl.semaphore_signal(
            barrier, inc=1, device_id=(grp, lax.rem(dev + t, n_dev)), device_id_type=MESH
        )
        return carry

    lax.fori_loop(1, n_dev, greet, 0)
    for k in hops:
        pl.semaphore_signal(barrier, inc=1, device_id=stream_device(k), device_id_type=MESH)

    def transpose_field(f):
        def tile(t, carry):
            lanes = pl.ds(multiple(t * LANES, LANES), LANES)
            turned = jnp.concatenate([inputs[f][b, :, lanes] for b in LANE_SLOTS], axis=0).T
            for jj in range(4):
                stages[f][pl.ds(4 * t + jj, SIDE, stride=SIDE), :] = turned[
                    SIDE * jj : SIDE * jj + SIDE
                ]
            return carry

        lax.fori_loop(0, 8, tile, 0)

    def spread(f):
        def send(t, carry):
            to = lax.rem(dev + t, n_dev)
            pltpu.make_async_remote_copy(
                src_ref=stages[f].at[pl.ds(multiple(to * rows, rows), rows)],
                dst_ref=mids[f].at[dev],
                send_sem=r["send_1"].at[f],
                recv_sem=r["recv_1"].at[f],
                device_id=(grp, to),
                device_id_type=MESH,
            ).start()
            return carry

        pltpu.make_async_copy(
            stages[f].at[pl.ds(multiple(dev * rows, rows), rows)], mids[f].at[dev],
            r["recv_1"].at[f],
        ).start()
        lax.fori_loop(1, n_dev, send, 0)

    group_of_lane = lax.broadcasted_iota(jnp.int32, (rows, LANES), 1) // SIDE

    def collect(f):
        pltpu.make_async_copy(mids[f], mids[f], r["recv_1"].at[f]).wait()
        mine = grids[f].at[pl.ds(H0 + dev * each, each), pl.ds(TOP, SIDE)]

        def assemble(to):
            base = (grp * n_dev + to) * 4
            made = None
            for place, slot in enumerate(LANE_SLOTS):
                old = lax.rem(source_ref[base + slot] // 4, n_dev)
                piece = mids[f][old]
                made = piece if made is None else jnp.where(group_of_lane == place, piece, made)
            asms[f][to] = made.reshape(each, SIDE, LANES)

        def send(t, carry):
            to = lax.rem(dev + t, n_dev)
            assemble(to)
            pltpu.make_async_remote_copy(
                src_ref=asms[f].at[to],
                dst_ref=mine,
                send_sem=r["send_2"].at[f],
                recv_sem=r["recv_2"].at[f],
                device_id=(grp, to),
                device_id_type=MESH,
            ).start()
            return carry

        lax.fori_loop(1, n_dev, send, 0)
        assemble(dev)
        pltpu.make_async_copy(asms[f].at[dev], mine, r["recv_2"].at[f]).start()

    def exchange(k, src, dst, send, recv):
        return pltpu.make_async_remote_copy(
            src_ref=src, dst_ref=dst, send_sem=send, recv_sem=recv,
            device_id=stream_device(k), device_id_type=MESH,
        )

    def start(copies):
        for copy in copies:
            copy.start()
        return copies

    def wait(copies):
        for copy in copies:
            copy.wait()

    def halos(x, own, halo, send, recv, *more):
        def part(lo):
            return x.at[(pl.ds(lo, halo), *more)]

        return [
            exchange(-1, part(halo), part(halo + own), send.at[0], recv.at[0]),
            exchange(1, part(own), part(0), send.at[1], recv.at[1]),
        ]

    def grid_halos(f):
        own = grids[f].at[pl.ds(H0, N0), pl.ds(TOP, SIDE)]
        pltpu.make_async_copy(own, own, r["recv_2"].at[f]).wait()
        body = pl.ds(TOP, SIDE)
        return start(halos(grids[f], N0, H0, r["send_h"].at[f], r["recv_h"].at[f], body))

    def grid_ready(f, copies):
        wait(copies)
        for edge, lo in ((0, 0), (count - 1, H0 + N0)):
            @pl.when(at == edge)
            def _():
                grids[f][pl.ds(lo, H0)] = jnp.zeros((H0, TALL, LANES), F32)

        def ghosts(ns):
            made = [(n, grids[f][n, BODY]) for n in ns]
            for n, v in made:
                grids[f][n, :TOP] = pltpu.roll(v[SIDE - TOP :], LANES // 2, 1)
                grids[f][n, TOP + SIDE :] = pltpu.roll(v[:TOP], LANES // 2, 1)

        steps(0, N0 + 2 * H0, 8, ghosts)

    def inside_of(own, halo):
        def inside(n):
            cell = at * own + n - halo
            return (cell >= 0) & (cell < count * own)

        return inside

    in0, in1 = inside_of(N0, H0), inside_of(N1, H1)
    in2, in3 = inside_of(N2, H2), inside_of(N3, H3)
    fine = Fine(SIDE, 2 * SIDE, 2 * SIDE, 1)
    lev1, lev2, lev3 = (Level(8, SIDE, SIDE, d) for d in (1, 2, 4))
    lane_f = lax.broadcasted_iota(jnp.int32, (LANES, LANES), 0)
    lane_c = lax.broadcasted_iota(jnp.int32, (LANES, LANES), 1)
    target = (lane_f // 64) * 64 + lax.rem(lane_f, 64) // 2
    down_m = [jnp.where(lane_c == target + 32 * jh, 0.5, 0.0).astype(F32) for jh in (0, 1)]
    target_t = (lane_c // 64) * 64 + lax.rem(lane_c, 64) // 2
    up_m = [jnp.where(lane_f == target_t + 32 * jh, 1.0, 0.0).astype(F32) for jh in (0, 1)]
    row8 = lax.broadcasted_iota(jnp.int32, (8, LANES), 0)
    lane8 = lax.broadcasted_iota(jnp.int32, (8, LANES), 1)
    tmp, half = r["tmp"], r["half"]

    def rows_halved(f, ms, totals):
        for i, total in enumerate(totals):
            tmp[i] = total
        made = [
            0.25 * (tmp[i, pl.ds(0, 16, stride=2), :] + tmp[i, pl.ds(1, 16, stride=2), :])
            for i in range(len(totals))
        ]
        for m, pairs in zip(ms, made):
            half[f, 0, m] = pairs[:8]
            half[f, 1, m] = pairs[8:]

    def lanes_halved(f):
        made = None
        for jh in (0, 1):
            part = jnp.dot(
                half[f, jh, :N1].reshape(N1 * 8, LANES), down_m[jh],
                precision=HIGHEST, preferred_element_type=F32,
            )
            made = part if made is None else made + part
        return made.reshape(N1, 8, LANES)

    def nu_pairs(ms):
        rows_halved(
            3, ms, [grids[0][H0 + 2 * m, BODY] + grids[0][H0 + 2 * m + 1, BODY] for m in ms]
        )

    def down_0(c):
        grid, s, a, b = grids[1 + c], r[f"s0{c}"], r[f"a0{c}"], r[f"b0{c}"]

        def first(ns):
            made = []
            for n in ns:
                g = [r["g0"][i, n] for i in range(6)]
                v = grid[n, BODY]
                scaled = r["w0"][n] * v
                made.append(
                    (n, scaled,
                     (1.0 - RELAX) * v + (scaled + gathered(fine, g, grid, BODY, n, v)))
                )
            for n, scaled, v in made:
                s[n] = scaled
                put(a, n, v)

        steps(1, N0 + 2 * H0 - 1, 2, first)
        sweep(
            fine, 2, N0 + 2 * H0 - 2, 2, r["g0"], [s], [a], lambda _, n, v: put(b, n, v), BODY
        )

        def pairs(ms):
            totals = []
            for m in ms:
                n = H0 + 2 * m
                [one] = residual(fine, n, r["g0"], r["iw0"], [s], [b], BODY)
                [two] = residual(fine, n + 1, r["g0"], r["iw0"], [s], [b], BODY)
                totals.append(one + two)
            rows_halved(c, ms, totals)

        steps(0, N1, 2, pairs)
        r["x1"][pl.ds(H1, N1), c] = lanes_halved(c)

    def blank(x, inside, ranges):
        for lo, hi in ranges:
            def planes(ns):
                made = [(n, jnp.where(inside(n), x[n], 0.0)) for n in ns]
                for n, v in made:
                    x[n] = v

            steps(lo, hi, 12, planes)

    def scaled(x, w, outs, lo, hi):
        def planes(ns):
            made = [(n, c, w[n] * x[n, c]) for n in ns for c in range(3)]
            for n, c, v in made:
                outs[c][n] = v

        steps(lo, hi, 8, planes)

    loads[0].wait()
    transpose_field(0)
    pl.semaphore_wait(barrier, n_dev - 1 + len(hops))
    spread(0)
    for f in range(1, 4):
        loads[f].wait()
        transpose_field(f)
        spread(f)
    for f in range(4):
        collect(f)

    grid_ready(0, grid_halos(0))
    weights(
        fine, DIFFUSION_NUMBER, 1, N0 + 2 * H0 - 1, 2, grids[0], BODY, in0, r["g0"], r["w0"],
        r["iw0"],
    )
    steps(0, N1, 4, nu_pairs)
    nu1, nu2, nu3 = r["nu1"], r["nu2"], r["nu3"]
    nu1[pl.ds(H1, N1)] = lanes_halved(3)
    moving = start(halos(nu1, N1, H1, r["send_e"].at[0], r["recv_e"].at[0]))
    waiting = grid_halos(1)

    wait(moving)
    blank(nu1, in1, [(0, H1), (H1 + N1, N1 + 2 * H1)])

    def nu_down(fine_nu, coarse_nu, halo_f, halo_c, d):
        def planes(ms):
            made = [
                (m, 0.125 * pair_sum(fine_nu[halo_f + 2 * m] + fine_nu[halo_f + 2 * m + 1], d))
                for m in ms
            ]
            for m, v in made:
                coarse_nu[halo_c + m] = v

        return planes

    steps(0, N2, 8, nu_down(nu1, nu2, H1, H2, 1))
    moving = start(halos(nu2, N2, H2, r["send_e"].at[1], r["recv_e"].at[1]))
    weights(
        lev1, DIFFUSION_NUMBER / 4, 1, N1 + 2 * H1 - 1, 6, nu1, ALL, in1, r["g1"], r["w1"], r["iw1"]
    )
    grid_ready(1, waiting)
    down_0(0)
    waiting = grid_halos(2)

    wait(moving)
    blank(nu2, in2, [(0, H2), (H2 + N2, N2 + 2 * H2)])
    steps(0, N3, 8, nu_down(nu2, nu3, H2, H3, 2))
    moving = start(
        [
            exchange(
                k, nu3.at[pl.ds(H3, N3)], nu3.at[pl.ds(H3 - k * N3, N3)],
                r["send_n3"].at[i], r["recv_n3"].at[i],
            )
            for i, k in enumerate(hops)
        ]
    )
    weights(
        lev2, DIFFUSION_NUMBER / 16, 1, N2 + 2 * H2 - 1, 6, nu2, ALL, in2, r["g2"], r["w2"],
        r["iw2"],
    )
    grid_ready(2, waiting)
    down_0(1)
    waiting = grid_halos(3)

    wait(moving)
    blank(nu3, in3, [(0, H3), (H3 + N3, N3 + 2 * H3)])
    planes3 = N3 + 2 * H3
    lo = H3 - 2 - (BOTTOM - 1)
    weights(
        lev3, DIFFUSION_NUMBER / 64, lo, planes3 - lo, 6, nu3, ALL, in3, r["g3"], r["w3"], r["iw3"]
    )
    grid_ready(3, waiting)
    down_0(2)

    x1, x2, x3 = r["x1"], r["x2"], r["x3"]
    s1, a1, b1 = three("s", 1), three("a", 1), three("b", 1)
    s2, a2, b2 = three("s", 2), three("a", 2), three("b", 2)
    s3, a3, b3 = three("s", 3), three("a", 3), three("b", 3)
    wait(start(halos(x1, N1, H1, r["send_e"].at[2], r["recv_e"].at[2])))
    blank(x1, in1, [(0, H1), (H1 + N1, N1 + 2 * H1)])
    scaled(x1, r["w1"], s1, 1, N1 + 2 * H1 - 1)
    sweep(lev1, 2, N1 + 2 * H1 - 2, 11, r["g1"], s1, s1, storing(a1))

    def down(level, ms, halo_f, halo_c, g, iw, s, a, x, d):
        made = []
        for m in ms:
            n = halo_f + 2 * m
            one = residual(level, n, g, iw, s, a)
            two = residual(level, n + 1, g, iw, s, a)
            for c in range(3):
                made.append((m, c, 0.125 * pair_sum(one[c] + two[c], d)))
        for m, c, v in made:
            x[halo_c + m, c] = v

    steps(0, N2, 4, lambda ms: down(lev1, ms, H1, H2, r["g1"], r["iw1"], s1, a1, x2, 1))

    place2 = lax.rem(row8, 2) * 2 + lax.rem(lane8, 2)
    pk2, pk3 = r["pk2"], r["pk3"]

    def pack_2(ms):
        made = []
        for m in ms:
            one = x2[H2 + m, 0]
            for c in (1, 2):
                one = jnp.where(place2 == c, x2[H2 + m, c], one)
            made.append((m, one))
        for m, one in made:
            pk2[H2 + m] = one

    steps(0, N2, 8, pack_2)
    wait(start(halos(pk2, N2, H2, r["send_e"].at[3], r["recv_e"].at[3])))

    def unpack_2(ns):
        made = []
        for n in ns:
            packed = jnp.where(in2(n), pk2[n], 0.0)
            for c in range(3):
                made.append((n, c, pair_sum(jnp.where(place2 == c, packed, 0.0), 1)))
        for n, c, v in made:
            x2[n, c] = v

    steps(0, H2, 6, unpack_2)
    steps(H2 + N2, N2 + 2 * H2, 6, unpack_2)
    scaled(x2, r["w2"], s2, 1, N2 + 2 * H2 - 1)
    sweep(lev2, 2, N2 + 2 * H2 - 2, 8, r["g2"], s2, s2, storing(a2))
    steps(0, N3, 4, lambda ms: down(lev2, ms, H2, H3, r["g2"], r["iw2"], s2, a2, x3, 2))

    row_of, lane_of = lax.rem(row8, 4), lax.rem(lane8, 4)
    made = None
    for m in range(N3):
        line = x3[H3 + m, 0]
        for c in (1, 2):
            line = jnp.where(lane_of == c, x3[H3 + m, c], line)
        made = line if made is None else jnp.where(row_of == m, line, made)
    pk3[REACH] = made
    wait(
        start(
            [
                exchange(k, pk3.at[REACH], pk3.at[REACH - k], r["send_r3"].at[i], r["recv_r3"].at[i])
                for i, k in enumerate(hops)
            ]
        )
    )

    def unpack_3(bs):
        made = []
        for b in bs:
            packed = pk3[b]
            for m in range(N3):
                n = N3 * b + m
                line = jnp.where((row_of == m) & in3(n), packed, 0.0)
                line = spread_rows(spread_rows(line, 1), 2)
                for c in range(3):
                    one = jnp.where(lane_of == c, line, 0.0)
                    made.append((n, c, spread_lanes(spread_lanes(one, 1), 2)))
        for n, c, v in made:
            x3[n, c] = v

    steps(0, REACH, 1, unpack_3)
    steps(REACH + 1, 2 * REACH + 1, 1, unpack_3)
    scaled(x3, r["w3"], s3, lo, planes3 - lo)
    src = s3
    for turn in range(1, BOTTOM):
        dst = a3 if turn % 2 else b3
        sweep(
            lev3, lo + turn, planes3 - lo - turn, 10, r["g3"], s3, src, storing(dst)
        )
        src = dst

    def add(bs, coarse, start_f, start_c):
        def pairs(ms):
            made = []
            for m in ms:
                for c in range(3):
                    more = coarse[c][start_c + m]
                    for twin in (0, 1):
                        n = start_f + 2 * m + twin
                        made.append((c, n, bs[c][n] + more))
            for c, n, v in made:
                bs[c][n] = v

        return pairs

    steps(0, (N2 + 8) // 2, 4, add(a2, src, H2 - 4, H3 - 2))
    sweep(lev2, 3, N2 + 2 * H2 - 3, 7, r["g2"], s2, a2, storing(b2))
    sweep(lev2, 4, N2 + 2 * H2 - 4, 6, r["g2"], s2, b2, storing(a2))
    steps(0, (N1 + 8) // 2, 4, add(a1, a2, H1 - 4, H2 - 2))
    sweep(lev1, 3, N1 + 2 * H1 - 3, 10, r["g1"], s1, a1, storing(b1))
    sweep(lev1, 4, N1 + 2 * H1 - 4, 9, r["g1"], s1, b1, storing(a1))

    wide = N1 + 2
    outs = (o_0, o_1, o_2)
    for c in range(3):
        coarse = a1[c][pl.ds(H1 - 1, wide)].reshape(wide * 8, LANES)
        for jh in (0, 1):
            half[c, jh] = jnp.dot(
                coarse, up_m[jh], precision=HIGHEST, preferred_element_type=F32
            ).reshape(wide, 8, LANES)

    for c in range(3):
        s, a, b = r[f"s0{c}"], r[f"a0{c}"], r[f"b0{c}"]

        def refined(ms, c=c, b=b):
            for i, m in enumerate(ms):
                for jh in (0, 1):
                    for twin in (0, 1):
                        tmp[3 * c + i, pl.ds(16 * jh + twin, 8, stride=2), :] = half[c, jh, m]
            made = []
            for i, m in enumerate(ms):
                for twin in (0, 1):
                    n = H0 - 2 + 2 * m + twin
                    made.append((n, b[n, BODY] + tmp[3 * c + i]))
            for n, v in made:
                put(b, n, v)

        steps(0, wide, 3, refined)
    s0, a0, b0 = three("s", 0), three("a", 0), three("b", 0)

    def to_a0(c, n, v):
        put(a0[c], n, v)

    def to_out(c, n, v):
        outs[c][n - H0] = v

    sweep(fine, 3, N0 + 2 * H0 - 3, 2, r["g0"], s0, b0, to_a0, BODY)
    sweep(fine, 4, N0 + 2 * H0 - 4, 2, r["g0"], s0, a0, to_out, BODY)

    for f in range(4):
        most = stages[f].at[pl.ds(0, (n_dev - 1) * rows)]
        pltpu.make_async_copy(most, most, r["send_1"].at[f]).wait()
        most = asms[f].at[pl.ds(0, n_dev - 1)]
        pltpu.make_async_copy(most, most, r["send_2"].at[f]).wait()


def whole(n_dev, source, velocity_old, viscosity_old):
    vmem = pl.BlockSpec(memory_space=pltpu.VMEM)
    anywhere = pl.BlockSpec(memory_space=pl.ANY)
    named = names_of_scratch(n_dev)
    return pl.pallas_call(
        functools.partial(whole_kernel, tuple(named)),
        out_shape=[jax.ShapeDtypeStruct((N0, SIDE, LANES), F32)] * 3,
        in_specs=[pl.BlockSpec(memory_space=pltpu.SMEM), anywhere, anywhere],
        out_specs=[vmem] * 3,
        scratch_shapes=list(named.values()),
        compiler_params=pltpu.CompilerParams(
            collective_id=0, has_side_effects=True, vmem_limit_bytes=VMEM_LIMIT
        ),
        name="whole",
    )(source, velocity_old, viscosity_old)


def blocks_kernel(e_0, e_1, e_2, out_ref):
    for c, e in enumerate((e_0, e_1, e_2)):
        def tile(t, carry):
            parts = [e[pl.ds(4 * t + jj, SIDE, stride=SIDE), :] for jj in range(4)]
            turned = jnp.concatenate(parts, axis=0).T
            lanes = pl.ds(multiple(t * LANES, LANES), LANES)
            for at, slot in enumerate(LANE_SLOTS):
                out_ref[slot, c, :, lanes] = turned[SIDE * at : SIDE * at + SIDE]
            return carry

        lax.fori_loop(0, 8, tile, 0)


def to_blocks(planes):
    vmem = pl.BlockSpec(memory_space=pltpu.VMEM)
    return pl.pallas_call(
        blocks_kernel,
        out_shape=jax.ShapeDtypeStruct((4, 3, SIDE, SIDE * SIDE), F32),
        in_specs=[vmem] * 3,
        out_specs=vmem,
        compiler_params=pltpu.CompilerParams(vmem_limit_bytes=VMEM_LIMIT),
        name="to_blocks",
    )(*[p.reshape(SIDE * SIDE, LANES) for p in planes])


def solution(mesh):
    n_dev = mesh.shape["dev"]

    def local(velocity_old, viscosity_old, source):
        return to_blocks(whole(n_dev, source, velocity_old, viscosity_old))

    return jax.shard_map(
        local,
        mesh=mesh,
        in_specs=(P(("grp", "dev"), None, None, None), P(("grp", "dev"), None, None), P()),
        out_specs=P(("grp", "dev"), None, None, None),
        check_vma=False,
    )
```

time: 1020 us -> 136 us (0.13); the launches traced: 1000 us -> 136 us
  local copies, waits for them, and re-layouts: 462 us -> 3.13 us
  waiting for transfers between devices: 219 us -> 0 us
  starting transfers between devices: 155 us -> 0 us
  Pallas kernels: 0 us -> 133 us
  other arithmetic: 115 us -> 0 us
  blocking collectives: 34.7 us -> 0 us
  between operations: 15.6 us -> 0.01 us
    reshape x10 -> x0, local copies, waits for them, and re-layouts: 348 us -> none  [the longest x3 171 us: coarsen(): grid.reshape(channels, length // 2, 2, width_y // 2, 2, width_y // 2, 2)]
    all_gather x2 -> x0, waiting for transfers between devices: 163 us -> none  [the longest x1 98.7 us: local(): lax.all_gather(velocity_old, 'dev', axis=0, tiled=True)]
    ppermute x54 -> x0, starting transfers between devices: 155 us -> none  [the longest x27 119 us: padded_2(): lax.ppermute(tail, axis, [(i, (i + 1) % count) for i in range(ends)])]
    pallas_call x0 -> x2, Pallas kernels: none -> 133 us  [the longest x1 129 us: whole(): pl.pallas_call(functools.partial(whole_kernel, tuple(named)), out_shape=[...]
    reduce_sum x6 -> x0, other arithmetic: 56.2 us -> none  [coarsen(): shaped.mean(axis=(2, 4, 6)).reshape(channels, length // 2, plane // 4)]
    ppermute x54 -> x0, waiting for transfers between devices: 55.2 us -> none  [the longest x27 54.4 us: padded_2(): lax.ppermute(head, axis, [((i + 1) % count, i) for i in range(ends)])]
    broadcast_in_dim x9 -> x0, local copies, waits for them, and re-layouts: 42.3 us -> none  [the longest x6 42.3 us: refine(): jnp.broadcast_to(shaped, (channels, length, 2, width_y, 2, width_y, 2))]
    all_gather x1 -> x0, blocking collectives: 34.7 us -> none  [group_bottom(): gathered = lax.all_gather(stacked, 'dev', axis=1, tiled=True)]
  transfers between devices with their start and end apart: 56 -> 0, of which waited for: 23 -> 0; matrix products, arithmetic and copies ran while one was open for 34% -> 0% of each run, Pallas kernels for 0% -> 0%
where the time goes in v2:
time: 136 us
  Pallas kernels  133 us (98%)
  local copies, waits for them, and re-layouts  3.13 us (2%)
    pallas_call x1, Pallas kernels, whole(): pl.pallas_call(functools.partial(whole_kernel, tuple(named)), out_shape=[...  129 us
    pallas_call x1, Pallas kernels, to_blocks(): pl.pallas_call(blocks_kernel, out_shape=jax.ShapeDtypeStruct((4, 3, SIDE,...  3.84 us
    unnamed x6, local copies, waits for them, and re-layouts  3.13 us

profile of v2, /device:TPU:0, one launch (start us, length us, event | category | flops | bytes accessed | tf_op | source)
XLA Modules:
  0.0 135.9 jit_solution(530076178626030339)
XLA Ops:
  0.0 0.0 copy-start
  0.0 1.4 %copy-done = f32[4,3,32,1024]{3,2,1,0:T(8,128)S(1)} copy-done((f32[4,3,32,1024]{3,2,1,0:T(8,128)S(1)}, f32[4,3,32,1024]{3,2,1,0:T(8,128)}, u32[]{:S(2)}) %copy-start) | copy-done | bytes 1572888
  1.4 0.0 copy-start.1
  1.4 1.0 copy-done.1
  2.5 0.0 copy-start.2
  2.5 0.7 copy-done.2
  3.1 128.9 %whole.1 = (f32[32,32,128]{2,1,0:T(8,128)S(1)}, f32[32,32,128]{2,1,0:T(8,128)S(1)}, f32[32,32,128]{2,1,0:T(8,128)S(1)}) custom-call(s32[512]{0:T(512)S(1)} %copy-done.2, f32[4,3,32,1024]{3,2,1,0:T(8,128)S(1)} %copy-done, f32[4,32,1024]{2,1,0:T(8,128)S(1)} %copy-done.1), custom_call_target="tpu_custom_call" | custom-call | tf_op jit(solution)/shard_map/whole/pallas_call | solution.py:718
  132.0 3.8 %to_blocks.1 = f32[4,3,32,1024]{3,2,1,0:T(8,128)} custom-call(f32[1024,128]{1,0:T(8,128)S(1)} %bitcast.3, f32[1024,128]{1,0:T(8,128)S(1)} %bitcast.4, f32[1024,128]{1,0:T(8,128)S(1)} %bitcast.5), custom_call_target="tpu_custom_call" | custom-call | tf_op jit(solution)/shard_map/to_blocks/pallas_call | solution.py:746
Async XLA Ops:
  0.0 1.4 %copy-start = (f32[4,3,32,1024]{3,2,1,0:T(8,128)S(1)}, f32[4,3,32,1024]{3,2,1,0:T(8,128)}, u32[]{:S(2)}) copy-start(f32[4,3,32,1024]{3,2,1,0:T(8,128)} %vel_hbm.1) | copy-start | bytes 4718596
  1.4 1.0 copy-start.1
  2.5 0.7 copy-start.2

commit v3 on v2

--- a/solution.py
+++ b/solution.py
@@ -14,6 +14,7 @@
 RELAX = 0.8
 BOTTOM = 8
 LANE_SLOTS = (0, 2, 1, 3)
+ANY = 64
 H0, H1, H2 = 4, 5, 6
 N0, N1, N2, N3 = 32, 16, 8, 4
 REACH = 3
@@ -60,16 +61,20 @@
 
 
 def steps(lo, hi, most, body):
-    size = max(t for t in range(1, most + 1) if (hi - lo) % t == 0)
+    count = hi - lo
+    size = -(-count // -(-count // most))
+    full, rest = divmod(count, size)
 
     def step(i, carry):
         body([lo + size * i + t for t in range(size)])
         return carry
 
-    if size == hi - lo:
-        step(0, 0)
+    if full == 1:
+        body(list(range(lo, lo + size)))
     else:
-        lax.fori_loop(0, (hi - lo) // size, step, 0)
+        lax.fori_loop(0, full, step, 0)
+    if rest:
+        body(list(range(hi - rest, hi)))
 
 
 class Level:
@@ -217,7 +222,7 @@
         named[f"s0{c}"] = vmem(n0, SIDE)
         named[f"a0{c}"] = vmem(n0, TALL)
         named[f"b0{c}"] = vmem(n0, TALL)
-    named |= {"tmp": vmem(3 * 3, SIDE), "half": vmem(4, 2, N1 + 2, 8)}
+    named |= {"tmp": vmem(9, SIDE), "half": vmem(4, 2, N1 + 2, 8)}
     for level, n in ((1, n1), (2, n2), (3, n3)):
         named |= {
             f"nu{level}": vmem(n, 8), f"x{level}": vmem(n, 3, 8), f"g{level}": vmem(6, n, 8),
@@ -271,16 +276,13 @@
         pl.semaphore_signal(barrier, inc=1, device_id=stream_device(k), device_id_type=MESH)
 
     def transpose_field(f):
-        def tile(t, carry):
-            lanes = pl.ds(multiple(t * LANES, LANES), LANES)
+        for t in range(8):
+            lanes = pl.ds(t * LANES, LANES)
             turned = jnp.concatenate([inputs[f][b, :, lanes] for b in LANE_SLOTS], axis=0).T
             for jj in range(4):
                 stages[f][pl.ds(4 * t + jj, SIDE, stride=SIDE), :] = turned[
                     SIDE * jj : SIDE * jj + SIDE
                 ]
-            return carry
-
-        lax.fori_loop(0, 8, tile, 0)
 
     def spread(f):
         def send(t, carry):
@@ -376,7 +378,7 @@
                 grids[f][n, :TOP] = pltpu.roll(v[SIDE - TOP :], LANES // 2, 1)
                 grids[f][n, TOP + SIDE :] = pltpu.roll(v[:TOP], LANES // 2, 1)
 
-        steps(0, N0 + 2 * H0, 8, ghosts)
+        steps(0, N0 + 2 * H0, 20, ghosts)
 
     def inside_of(own, halo):
         def inside(n):
@@ -442,9 +444,9 @@
                 s[n] = scaled
                 put(a, n, v)
 
-        steps(1, N0 + 2 * H0 - 1, 2, first)
+        steps(1, N0 + 2 * H0 - 1, 19, first)
         sweep(
-            fine, 2, N0 + 2 * H0 - 2, 2, r["g0"], [s], [a], lambda _, n, v: put(b, n, v), BODY
+            fine, 2, N0 + 2 * H0 - 2, 18, r["g0"], [s], [a], lambda _, n, v: put(b, n, v), BODY
         )
 
         def pairs(ms):
@@ -456,7 +458,7 @@
                 totals.append(one + two)
             rows_halved(c, ms, totals)
 
-        steps(0, N1, 2, pairs)
+        steps(0, N1, 8, pairs)
         r["x1"][pl.ds(H1, N1), c] = lanes_halved(c)
 
     def blank(x, inside, ranges):
@@ -474,32 +476,9 @@
             for n, c, v in made:
                 outs[c][n] = v
 
-        steps(lo, hi, 8, planes)
-
-    loads[0].wait()
-    transpose_field(0)
-    pl.semaphore_wait(barrier, n_dev - 1 + len(hops))
-    spread(0)
-    for f in range(1, 4):
-        loads[f].wait()
-        transpose_field(f)
-        spread(f)
-    for f in range(4):
-        collect(f)
-
-    grid_ready(0, grid_halos(0))
-    weights(
-        fine, DIFFUSION_NUMBER, 1, N0 + 2 * H0 - 1, 2, grids[0], BODY, in0, r["g0"], r["w0"],
-        r["iw0"],
-    )
-    steps(0, N1, 4, nu_pairs)
+        steps(lo, hi, ANY, planes)
+
     nu1, nu2, nu3 = r["nu1"], r["nu2"], r["nu3"]
-    nu1[pl.ds(H1, N1)] = lanes_halved(3)
-    moving = start(halos(nu1, N1, H1, r["send_e"].at[0], r["recv_e"].at[0]))
-    waiting = grid_halos(1)
-
-    wait(moving)
-    blank(nu1, in1, [(0, H1), (H1 + N1, N1 + 2 * H1)])
 
     def nu_down(fine_nu, coarse_nu, halo_f, halo_c, d):
         def planes(ms):
@@ -512,15 +491,41 @@
 
         return planes
 
+    def staged(f):
+        loads[f].wait()
+        transpose_field(f)
+
+    staged(0)
+    pl.semaphore_wait(barrier, n_dev - 1 + len(hops))
+    spread(0)
+    staged(1)
+    spread(1)
+    staged(2)
+    collect(0)
+    spread(2)
+    staged(3)
+    moving = grid_halos(0)
+    collect(1)
+    spread(3)
+
+    grid_ready(0, moving)
+    steps(0, N1, 8, nu_pairs)
+    nu1[pl.ds(H1, N1)] = lanes_halved(3)
+    moving = start(halos(nu1, N1, H1, r["send_e"].at[0], r["recv_e"].at[0]))
+    weights(
+        fine, DIFFUSION_NUMBER, 1, N0 + 2 * H0 - 1, 10, grids[0], BODY, in0, r["g0"], r["w0"],
+        r["iw0"],
+    )
+    collect(2)
+    waiting = grid_halos(1)
+    wait(moving)
+    blank(nu1, in1, [(0, H1), (H1 + N1, N1 + 2 * H1)])
     steps(0, N2, 8, nu_down(nu1, nu2, H1, H2, 1))
     moving = start(halos(nu2, N2, H2, r["send_e"].at[1], r["recv_e"].at[1]))
+    collect(3)
     weights(
-        lev1, DIFFUSION_NUMBER / 4, 1, N1 + 2 * H1 - 1, 6, nu1, ALL, in1, r["g1"], r["w1"], r["iw1"]
-    )
-    grid_ready(1, waiting)
-    down_0(0)
-    waiting = grid_halos(2)
-
+        lev1, DIFFUSION_NUMBER / 4, 1, N1 + 2 * H1 - 1, ANY, nu1, ALL, in1, r["g1"], r["w1"], r["iw1"]
+    )
     wait(moving)
     blank(nu2, in2, [(0, H2), (H2 + N2, N2 + 2 * H2)])
     steps(0, N3, 8, nu_down(nu2, nu3, H2, H3, 2))
@@ -534,20 +539,22 @@
         ]
     )
     weights(
-        lev2, DIFFUSION_NUMBER / 16, 1, N2 + 2 * H2 - 1, 6, nu2, ALL, in2, r["g2"], r["w2"],
+        lev2, DIFFUSION_NUMBER / 16, 1, N2 + 2 * H2 - 1, ANY, nu2, ALL, in2, r["g2"], r["w2"],
         r["iw2"],
     )
-    grid_ready(2, waiting)
-    down_0(1)
-    waiting = grid_halos(3)
-
+    grid_ready(1, waiting)
+    waiting = grid_halos(2)
+    down_0(0)
     wait(moving)
     blank(nu3, in3, [(0, H3), (H3 + N3, N3 + 2 * H3)])
     planes3 = N3 + 2 * H3
     lo = H3 - 2 - (BOTTOM - 1)
     weights(
-        lev3, DIFFUSION_NUMBER / 64, lo, planes3 - lo, 6, nu3, ALL, in3, r["g3"], r["w3"], r["iw3"]
-    )
+        lev3, DIFFUSION_NUMBER / 64, lo, planes3 - lo, ANY, nu3, ALL, in3, r["g3"], r["w3"], r["iw3"]
+    )
+    grid_ready(2, waiting)
+    waiting = grid_halos(3)
+    down_0(1)
     grid_ready(3, waiting)
     down_0(2)
 
@@ -558,7 +565,7 @@
     wait(start(halos(x1, N1, H1, r["send_e"].at[2], r["recv_e"].at[2])))
     blank(x1, in1, [(0, H1), (H1 + N1, N1 + 2 * H1)])
     scaled(x1, r["w1"], s1, 1, N1 + 2 * H1 - 1)
-    sweep(lev1, 2, N1 + 2 * H1 - 2, 11, r["g1"], s1, s1, storing(a1))
+    sweep(lev1, 2, N1 + 2 * H1 - 2, ANY, r["g1"], s1, s1, storing(a1))
 
     def down(level, ms, halo_f, halo_c, g, iw, s, a, x, d):
         made = []
@@ -571,7 +578,7 @@
         for m, c, v in made:
             x[halo_c + m, c] = v
 
-    steps(0, N2, 4, lambda ms: down(lev1, ms, H1, H2, r["g1"], r["iw1"], s1, a1, x2, 1))
+    steps(0, N2, ANY, lambda ms: down(lev1, ms, H1, H2, r["g1"], r["iw1"], s1, a1, x2, 1))
 
     place2 = lax.rem(row8, 2) * 2 + lax.rem(lane8, 2)
     pk2, pk3 = r["pk2"], r["pk3"]
@@ -601,7 +608,7 @@
     steps(0, H2, 6, unpack_2)
     steps(H2 + N2, N2 + 2 * H2, 6, unpack_2)
     scaled(x2, r["w2"], s2, 1, N2 + 2 * H2 - 1)
-    sweep(lev2, 2, N2 + 2 * H2 - 2, 8, r["g2"], s2, s2, storing(a2))
+    sweep(lev2, 2, N2 + 2 * H2 - 2, ANY, r["g2"], s2, s2, storing(a2))
     steps(0, N3, 4, lambda ms: down(lev2, ms, H2, H3, r["g2"], r["iw2"], s2, a2, x3, 2))
 
     row_of, lane_of = lax.rem(row8, 4), lax.rem(lane8, 4)
@@ -635,14 +642,14 @@
         for n, c, v in made:
             x3[n, c] = v
 
-    steps(0, REACH, 1, unpack_3)
-    steps(REACH + 1, 2 * REACH + 1, 1, unpack_3)
+    steps(0, REACH, ANY, unpack_3)
+    steps(REACH + 1, 2 * REACH + 1, ANY, unpack_3)
     scaled(x3, r["w3"], s3, lo, planes3 - lo)
     src = s3
     for turn in range(1, BOTTOM):
         dst = a3 if turn % 2 else b3
         sweep(
-            lev3, lo + turn, planes3 - lo - turn, 10, r["g3"], s3, src, storing(dst)
+            lev3, lo + turn, planes3 - lo - turn, ANY, r["g3"], s3, src, storing(dst)
         )
         src = dst
 
@@ -660,12 +667,12 @@
 
         return pairs
 
-    steps(0, (N2 + 8) // 2, 4, add(a2, src, H2 - 4, H3 - 2))
-    sweep(lev2, 3, N2 + 2 * H2 - 3, 7, r["g2"], s2, a2, storing(b2))
-    sweep(lev2, 4, N2 + 2 * H2 - 4, 6, r["g2"], s2, b2, storing(a2))
-    steps(0, (N1 + 8) // 2, 4, add(a1, a2, H1 - 4, H2 - 2))
-    sweep(lev1, 3, N1 + 2 * H1 - 3, 10, r["g1"], s1, a1, storing(b1))
-    sweep(lev1, 4, N1 + 2 * H1 - 4, 9, r["g1"], s1, b1, storing(a1))
+    steps(0, (N2 + 8) // 2, ANY, add(a2, src, H2 - 4, H3 - 2))
+    sweep(lev2, 3, N2 + 2 * H2 - 3, ANY, r["g2"], s2, a2, storing(b2))
+    sweep(lev2, 4, N2 + 2 * H2 - 4, ANY, r["g2"], s2, b2, storing(a2))
+    steps(0, (N1 + 8) // 2, ANY, add(a1, a2, H1 - 4, H2 - 2))
+    sweep(lev1, 3, N1 + 2 * H1 - 3, ANY, r["g1"], s1, a1, storing(b1))
+    sweep(lev1, 4, N1 + 2 * H1 - 4, ANY, r["g1"], s1, b1, storing(a1))
 
     wide = N1 + 2
     outs = (o_0, o_1, o_2)
@@ -683,26 +690,33 @@
             for i, m in enumerate(ms):
                 for jh in (0, 1):
                     for twin in (0, 1):
-                        tmp[3 * c + i, pl.ds(16 * jh + twin, 8, stride=2), :] = half[c, jh, m]
+                        tmp[i, pl.ds(16 * jh + twin, 8, stride=2), :] = half[c, jh, m]
             made = []
             for i, m in enumerate(ms):
                 for twin in (0, 1):
                     n = H0 - 2 + 2 * m + twin
-                    made.append((n, b[n, BODY] + tmp[3 * c + i]))
+                    made.append((n, b[n, BODY] + tmp[i]))
             for n, v in made:
                 put(b, n, v)
 
-        steps(0, wide, 3, refined)
+        steps(0, wide, 9, refined)
     s0, a0, b0 = three("s", 0), three("a", 0), three("b", 0)
 
-    def to_a0(c, n, v):
+    def to_a0(c, _, n, v):
         put(a0[c], n, v)
 
-    def to_out(c, n, v):
+    def to_out(c, _, n, v):
         outs[c][n - H0] = v
 
-    sweep(fine, 3, N0 + 2 * H0 - 3, 2, r["g0"], s0, b0, to_a0, BODY)
-    sweep(fine, 4, N0 + 2 * H0 - 4, 2, r["g0"], s0, a0, to_out, BODY)
+    for c in range(3):
+        sweep(
+            fine, 3, N0 + 2 * H0 - 3, 17, r["g0"], [s0[c]], [b0[c]],
+            functools.partial(to_a0, c), BODY,
+        )
+        sweep(
+            fine, 4, N0 + 2 * H0 - 4, 16, r["g0"], [s0[c]], [a0[c]],
+            functools.partial(to_out, c), BODY,
+        )
 
     for f in range(4):
         most = stages[f].at[pl.ds(0, (n_dev - 1) * rows)]
@@ -730,15 +744,11 @@
 
 def blocks_kernel(e_0, e_1, e_2, out_ref):
     for c, e in enumerate((e_0, e_1, e_2)):
-        def tile(t, carry):
+        for t in range(8):
             parts = [e[pl.ds(4 * t + jj, SIDE, stride=SIDE), :] for jj in range(4)]
             turned = jnp.concatenate(parts, axis=0).T
-            lanes = pl.ds(multiple(t * LANES, LANES), LANES)
             for at, slot in enumerate(LANE_SLOTS):
-                out_ref[slot, c, :, lanes] = turned[SIDE * at : SIDE * at + SIDE]
-            return carry
-
-        lax.fori_loop(0, 8, tile, 0)
+                out_ref[slot, c, :, pl.ds(t * LANES, LANES)] = turned[SIDE * at : SIDE * at + SIDE]
 
 
 def to_blocks(planes):

time: 136 us -> 103 us (0.76)
  Pallas kernels: 133 us -> 99.8 us
    pallas_call x1, Pallas kernels: 129 us -> 97.8 us  [whole(): pl.pallas_call(functools.partial(whole_kernel, tuple(named)), out_shape=[...]
    pallas_call x1, Pallas kernels: 3.84 us -> 2.07 us  [to_blocks(): pl.pallas_call(blocks_kernel, out_shape=jax.ShapeDtypeStruct((4, 3, SIDE,...]
where the time goes in v3:
time: 103 us
  Pallas kernels  99.8 us (97%)
  local copies, waits for them, and re-layouts  3.13 us (3%)
    pallas_call x1, Pallas kernels, whole(): pl.pallas_call(functools.partial(whole_kernel, tuple(named)), out_shape=[...  97.8 us
    unnamed x6, local copies, waits for them, and re-layouts  3.13 us
    pallas_call x1, Pallas kernels, to_blocks(): pl.pallas_call(blocks_kernel, out_shape=jax.ShapeDtypeStruct((4, 3, SIDE,...  2.07 us

profile of v3, /device:TPU:0, one launch (start us, length us, event | category | flops | bytes accessed | tf_op | source)
XLA Modules:
  0.0 103.0 jit_solution(18160896155061767136)
XLA Ops:
  0.0 0.0 copy-start
  0.0 1.4 %copy-done = f32[4,3,32,1024]{3,2,1,0:T(8,128)S(1)} copy-done((f32[4,3,32,1024]{3,2,1,0:T(8,128)S(1)}, f32[4,3,32,1024]{3,2,1,0:T(8,128)}, u32[]{:S(2)}) %copy-start) | copy-done | bytes 1572888
  1.4 0.0 copy-start.1
  1.4 1.0 %copy-done.1 = f32[4,32,1024]{2,1,0:T(8,128)S(1)} copy-done((f32[4,32,1024]{2,1,0:T(8,128)S(1)}, f32[4,32,1024]{2,1,0:T(8,128)}, u32[]{:S(2)}) %copy-start.1) | copy-done | bytes 524312
  2.5 0.0 copy-start.2
  2.5 0.7 copy-done.2
  3.1 97.8 %whole.1 = (f32[32,32,128]{2,1,0:T(8,128)S(1)}, f32[32,32,128]{2,1,0:T(8,128)S(1)}, f32[32,32,128]{2,1,0:T(8,128)S(1)}) custom-call(s32[512]{0:T(512)S(1)} %copy-done.2, f32[4,3,32,1024]{3,2,1,0:T(8,128)S(1)} %copy-done, f32[4,32,1024]{2,1,0:T(8,128)S(1)} %copy-done.1), custom_call_target="tpu_custom_call" | custom-call | tf_op jit(solution)/shard_map/whole/pallas_call | solution.py:732
  100.9 2.1 %to_blocks.1 = f32[4,3,32,1024]{3,2,1,0:T(8,128)} custom-call(f32[1024,128]{1,0:T(8,128)S(1)} %bitcast.3, f32[1024,128]{1,0:T(8,128)S(1)} %bitcast.4, f32[1024,128]{1,0:T(8,128)S(1)} %bitcast.5), custom_call_target="tpu_custom_call" | custom-call | tf_op jit(solution)/shard_map/to_blocks/pallas_call | solution.py:756
Async XLA Ops:
  0.0 1.4 %copy-start = (f32[4,3,32,1024]{3,2,1,0:T(8,128)S(1)}, f32[4,3,32,1024]{3,2,1,0:T(8,128)}, u32[]{:S(2)}) copy-start(f32[4,3,32,1024]{3,2,1,0:T(8,128)} %vel_hbm.1) | copy-start | bytes 4718596
  1.4 1.0 %copy-start.1 = (f32[4,32,1024]{2,1,0:T(8,128)S(1)}, f32[4,32,1024]{2,1,0:T(8,128)}, u32[]{:S(2)}) copy-start(f32[4,32,1024]{2,1,0:T(8,128)} %vis_hbm.1) | copy-start | bytes 1572868
  2.5 0.7 copy-start.2

commit v4 on v3

--- a/solution.py
+++ b/solution.py
@@ -15,10 +15,10 @@
 BOTTOM = 8
 LANE_SLOTS = (0, 2, 1, 3)
 ANY = 64
-H0, H1, H2 = 4, 5, 6
+H0, H1 = 4, 5
 N0, N1, N2, N3 = 32, 16, 8, 4
 REACH = 3
-H3 = REACH * N3
+H2, H3 = REACH * N2, REACH * N3
 VMEM_LIMIT = 48 * 1024 * 1024
 MESH = pl.DeviceIdType.MESH
 HIGHEST = lax.Precision.HIGHEST
@@ -36,6 +36,7 @@
     return (at // n_dev, lax.rem(at, n_dev))
 
 
+STRIDE_TILES = 8
 TOP = 8
 TALL = SIDE + 2 * TOP
 BODY = slice(TOP, TOP + SIDE)
@@ -200,7 +201,6 @@
 
 
 def names_of_scratch(n_dev):
-    each = SIDE // n_dev
     n0, n1, n2, n3 = N0 + 2 * H0, N1 + 2 * H1, N2 + 2 * H2, N3 + 2 * H3
 
     def vmem(*shape):
@@ -214,8 +214,8 @@
         named[f"vel{c}"] = pltpu.VMEM((4, SIDE, SIDE * SIDE), F32)
     for f in range(4):
         named[f"stage{f}"] = vmem(SIDE * SIDE)
-        named[f"mid{f}"] = vmem(n_dev, each * SIDE)
-        named[f"asm{f}"] = vmem(n_dev, each, SIDE)
+        named[f"mid{f}"] = vmem(n_dev, STRIDE_TILES, 8)
+        named[f"asm{f}"] = vmem(n_dev + 2, STRIDE_TILES + 2, 8)
         named[f"grid{f}"] = vmem(n0, TALL)
     named |= {"g0": vmem(6, n0, SIDE), "w0": vmem(n0, SIDE), "iw0": vmem(n0, SIDE)}
     for c in range(3):
@@ -225,18 +225,19 @@
     named |= {"tmp": vmem(9, SIDE), "half": vmem(4, 2, N1 + 2, 8)}
     for level, n in ((1, n1), (2, n2), (3, n3)):
         named |= {
-            f"nu{level}": vmem(n, 8), f"x{level}": vmem(n, 3, 8), f"g{level}": vmem(6, n, 8),
+            f"nu{level}": vmem(n, 8), f"g{level}": vmem(6, n, 8),
             f"w{level}": vmem(n, 8), f"iw{level}": vmem(n, 8),
         }
         for c in range(3):
-            for kind in "sab":
+            for kind in "xsab":
                 named[f"{kind}{level}{c}"] = vmem(n, 8)
+    for f in range(4):
+        named[f"pack{f}"] = vmem(2 * REACH + 1, 2, 8)
     named |= {
-        "pk2": vmem(n2, 8), "pk3": vmem(2 * REACH + 1, 8), "in_sem": dma(4),
+        "in_sem": dma(4),
         "send_1": dma(4), "recv_1": dma(4), "send_2": dma(4), "recv_2": dma(4),
-        "send_h": dma(4, 2), "recv_h": dma(4, 2), "send_e": dma(5, 2), "recv_e": dma(5, 2),
-        "send_n3": dma(2 * REACH), "recv_n3": dma(2 * REACH),
-        "send_r3": dma(2 * REACH), "recv_r3": dma(2 * REACH),
+        "send_e": dma(4, 2), "recv_e": dma(4, 2),
+        "send_p": dma(4, 2 * REACH), "recv_p": dma(4, 2 * REACH),
     }
     return named
 
@@ -246,15 +247,11 @@
     grp, dev, n_grp, n_dev = positions()
     at = grp * n_dev + dev
     count = n_grp * n_dev
-    each = SIDE // n_dev
-    rows = each * SIDE
+    phase, rg = dev // 4, lax.rem(dev, 4)
     hops = [k for k in range(-REACH, REACH + 1) if k]
     stages, mids = [r[f"stage{f}"] for f in range(4)], [r[f"mid{f}"] for f in range(4)]
     asms, grids = [r[f"asm{f}"] for f in range(4)], [r[f"grid{f}"] for f in range(4)]
     inputs = [r["vis"]] + [r[f"vel{c}"] for c in range(3)]
-
-    def three(kind, level):
-        return [r[f"{kind}{level}{c}"] for c in range(3)]
 
     loads = [pltpu.make_async_copy(vis_hbm, inputs[0], r["in_sem"].at[0])]
     loads += [
@@ -272,6 +269,29 @@
         return carry
 
     lax.fori_loop(1, n_dev, greet, 0)
+    next_first = (lax.rem(grp + 1, n_grp), 0)
+    before_last = (lax.rem(grp + n_grp - 1, n_grp), n_dev - 1)
+    for beside in (next_first, before_last):
+        pl.semaphore_signal(barrier, inc=1, device_id=beside, device_id_type=MESH)
+
+    @pl.when(dev == 0)
+    def _():
+        def back(t, carry):
+            pl.semaphore_signal(
+                barrier, inc=1, device_id=(before_last[0], t), device_id_type=MESH
+            )
+            return carry
+
+        lax.fori_loop(0, n_dev, back, 0)
+
+    @pl.when(dev == n_dev - 1)
+    def _():
+        def onward(t, carry):
+            pl.semaphore_signal(barrier, inc=1, device_id=(next_first[0], t), device_id_type=MESH)
+            return carry
+
+        lax.fori_loop(0, n_dev, onward, 0)
+
     for k in hops:
         pl.semaphore_signal(barrier, inc=1, device_id=stream_device(k), device_id_type=MESH)
 
@@ -285,10 +305,12 @@
                 ]
 
     def spread(f):
+        tiles = stages[f].reshape(STRIDE_TILES, 4, 4, 8, LANES)
+
         def send(t, carry):
             to = lax.rem(dev + t, n_dev)
             pltpu.make_async_remote_copy(
-                src_ref=stages[f].at[pl.ds(multiple(to * rows, rows), rows)],
+                src_ref=tiles.at[:, to // 4, lax.rem(to, 4)],
                 dst_ref=mids[f].at[dev],
                 send_sem=r["send_1"].at[f],
                 recv_sem=r["recv_1"].at[f],
@@ -297,43 +319,71 @@
             ).start()
             return carry
 
-        pltpu.make_async_copy(
-            stages[f].at[pl.ds(multiple(dev * rows, rows), rows)], mids[f].at[dev],
-            r["recv_1"].at[f],
-        ).start()
+        pltpu.make_async_copy(tiles.at[:, phase, rg], mids[f].at[dev], r["recv_1"].at[f]).start()
         lax.fori_loop(1, n_dev, send, 0)
 
-    group_of_lane = lax.broadcasted_iota(jnp.int32, (rows, LANES), 1) // SIDE
+    group_of_lane = lax.broadcasted_iota(jnp.int32, (STRIDE_TILES, 8, LANES), 2) // SIDE
+    far = STRIDE_TILES + 1
 
     def collect(f):
         pltpu.make_async_copy(mids[f], mids[f], r["recv_1"].at[f]).wait()
-        mine = grids[f].at[pl.ds(H0 + dev * each, each), pl.ds(TOP, SIDE)]
-
-        def assemble(to):
-            base = (grp * n_dev + to) * 4
+        grid = grids[f].reshape(STRIDE_TILES + 2, 4, TALL, LANES)
+        asm = asms[f]
+
+        def assemble(d, carry):
+            base = (grp * n_dev + d) * 4
             made = None
             for place, slot in enumerate(LANE_SLOTS):
                 old = lax.rem(source_ref[base + slot] // 4, n_dev)
                 piece = mids[f][old]
                 made = piece if made is None else jnp.where(group_of_lane == place, piece, made)
-            asms[f][to] = made.reshape(each, SIDE, LANES)
+            asm[d + 1, 1:far] = made
+            asm[d + 2, 0] = made[STRIDE_TILES - 1]
+            asm[d, far] = made[0]
+            return carry
+
+        for d in range(n_dev):
+            assemble(d, 0)
+
+        def parts(d, lo, hi):
+            places = pl.ds(lo, hi - lo)
+            return (
+                asm.at[d + 1, places],
+                grid.at[places, phase, pl.ds(multiple(TOP + 8 * rg, 8), 8)],
+            )
+
+        def remote(d, lo, hi, target):
+            src, dst = parts(d, lo, hi)
+            pltpu.make_async_remote_copy(
+                src_ref=src, dst_ref=dst, send_sem=r["send_2"].at[f], recv_sem=r["recv_2"].at[f],
+                device_id=target, device_id_type=MESH,
+            ).start()
+
+        def local(d, lo, hi, target):
+            src, dst = parts(d, lo, hi)
+            pltpu.make_async_copy(src, dst, r["recv_2"].at[f]).start()
+
+        def to_device(copy, d):
+            @pl.when(d == 0)
+            def _():
+                copy(d, 1, far + 1, (grp, d))
+
+            @pl.when(d == n_dev - 1)
+            def _():
+                copy(d, 0, far, (grp, d))
+
+            @pl.when((d > 0) & (d < n_dev - 1))
+            def _():
+                copy(d, 0, far + 1, (grp, d))
 
         def send(t, carry):
-            to = lax.rem(dev + t, n_dev)
-            assemble(to)
-            pltpu.make_async_remote_copy(
-                src_ref=asms[f].at[to],
-                dst_ref=mine,
-                send_sem=r["send_2"].at[f],
-                recv_sem=r["recv_2"].at[f],
-                device_id=(grp, to),
-                device_id_type=MESH,
-            ).start()
+            to_device(remote, lax.rem(dev + t, n_dev))
             return carry
 
         lax.fori_loop(1, n_dev, send, 0)
-        assemble(dev)
-        pltpu.make_async_copy(asms[f].at[dev], mine, r["recv_2"].at[f]).start()
+        to_device(local, dev)
+        remote(n_dev, 0, 1, next_first)
+        remote(-1, far, far + 1, before_last)
 
     def exchange(k, src, dst, send, recv):
         return pltpu.make_async_remote_copy(
@@ -359,14 +409,9 @@
             exchange(1, part(own), part(0), send.at[1], recv.at[1]),
         ]
 
-    def grid_halos(f):
-        own = grids[f].at[pl.ds(H0, N0), pl.ds(TOP, SIDE)]
-        pltpu.make_async_copy(own, own, r["recv_2"].at[f]).wait()
-        body = pl.ds(TOP, SIDE)
-        return start(halos(grids[f], N0, H0, r["send_h"].at[f], r["recv_h"].at[f], body))
-
-    def grid_ready(f, copies):
-        wait(copies)
+    def grid_ready(f):
+        body = grids[f].at[:, pl.ds(TOP, SIDE)]
+        pltpu.make_async_copy(body, body, r["recv_2"].at[f]).wait()
         for edge, lo in ((0, 0), (count - 1, H0 + N0)):
             @pl.when(at == edge)
             def _():
@@ -459,7 +504,7 @@
             rows_halved(c, ms, totals)
 
         steps(0, N1, 8, pairs)
-        r["x1"][pl.ds(H1, N1), c] = lanes_halved(c)
+        r[f"x1{c}"][pl.ds(H1, N1)] = lanes_halved(c)
 
     def blank(x, inside, ranges):
         for lo, hi in ranges:
@@ -470,13 +515,50 @@
 
             steps(lo, hi, 12, planes)
 
-    def scaled(x, w, outs, lo, hi):
+    def scaled(x, w, out, lo, hi):
         def planes(ns):
-            made = [(n, c, w[n] * x[n, c]) for n in ns for c in range(3)]
-            for n, c, v in made:
-                outs[c][n] = v
+            made = [(n, w[n] * x[n]) for n in ns]
+            for n, v in made:
+                out[n] = v
 
         steps(lo, hi, ANY, planes)
+
+    place = lax.rem(row8, 2) * 2 + lax.rem(lane8, 2)
+
+    def pack(f, x):
+        for h in range(N2 // 4):
+            made = x[H2 + 4 * h]
+            for p in range(1, 4):
+                made = jnp.where(place == p, x[H2 + 4 * h + p], made)
+            r[f"pack{f}"][REACH, h] = made
+        packed = r[f"pack{f}"]
+        return start(
+            [
+                exchange(
+                    k, packed.at[REACH], packed.at[REACH - k],
+                    r["send_p"].at[f, i], r["recv_p"].at[f, i],
+                )
+                for i, k in enumerate(hops)
+            ]
+        )
+
+    def unpack(f, x, moving):
+        wait(moving)
+
+        def blocks(bs):
+            made = []
+            for b in bs:
+                for h in range(N2 // 4):
+                    packed = r[f"pack{f}"][b, h]
+                    for p in range(4):
+                        n = N2 * b + 4 * h + p
+                        one = jnp.where((place == p) & in2(n), packed, 0.0)
+                        made.append((n, pair_sum(one, 1)))
+            for n, v in made:
+                x[n] = v
+
+        steps(0, REACH, ANY, blocks)
+        steps(REACH + 1, 2 * REACH + 1, ANY, blocks)
 
     nu1, nu2, nu3 = r["nu1"], r["nu2"], r["nu3"]
 
@@ -491,202 +573,119 @@
 
         return planes
 
+    def to_level_1(c):
+        send, recv = r["send_e"].at[1 + c], r["recv_e"].at[1 + c]
+        return start(halos(r[f"x1{c}"], N1, H1, send, recv))
+
     def staged(f):
         loads[f].wait()
         transpose_field(f)
 
-    staged(0)
-    pl.semaphore_wait(barrier, n_dev - 1 + len(hops))
+    for f in range(4):
+        staged(f)
+    ends = jnp.where((dev == 0) | (dev == n_dev - 1), n_dev, 0)
+    pl.semaphore_wait(barrier, n_dev - 1 + len(hops) + 2 + ends)
     spread(0)
-    staged(1)
     spread(1)
-    staged(2)
     collect(0)
     spread(2)
-    staged(3)
-    moving = grid_halos(0)
     collect(1)
     spread(3)
-
-    grid_ready(0, moving)
+    collect(2)
+
+    grid_ready(0)
     steps(0, N1, 8, nu_pairs)
     nu1[pl.ds(H1, N1)] = lanes_halved(3)
     moving = start(halos(nu1, N1, H1, r["send_e"].at[0], r["recv_e"].at[0]))
+    collect(3)
     weights(
         fine, DIFFUSION_NUMBER, 1, N0 + 2 * H0 - 1, 10, grids[0], BODY, in0, r["g0"], r["w0"],
         r["iw0"],
     )
-    collect(2)
-    waiting = grid_halos(1)
     wait(moving)
     blank(nu1, in1, [(0, H1), (H1 + N1, N1 + 2 * H1)])
     steps(0, N2, 8, nu_down(nu1, nu2, H1, H2, 1))
-    moving = start(halos(nu2, N2, H2, r["send_e"].at[1], r["recv_e"].at[1]))
-    collect(3)
+    moving = pack(3, nu2)
     weights(
         lev1, DIFFUSION_NUMBER / 4, 1, N1 + 2 * H1 - 1, ANY, nu1, ALL, in1, r["g1"], r["w1"], r["iw1"]
     )
-    wait(moving)
-    blank(nu2, in2, [(0, H2), (H2 + N2, N2 + 2 * H2)])
-    steps(0, N3, 8, nu_down(nu2, nu3, H2, H3, 2))
-    moving = start(
-        [
-            exchange(
-                k, nu3.at[pl.ds(H3, N3)], nu3.at[pl.ds(H3 - k * N3, N3)],
-                r["send_n3"].at[i], r["recv_n3"].at[i],
-            )
-            for i, k in enumerate(hops)
-        ]
-    )
-    weights(
-        lev2, DIFFUSION_NUMBER / 16, 1, N2 + 2 * H2 - 1, ANY, nu2, ALL, in2, r["g2"], r["w2"],
-        r["iw2"],
-    )
-    grid_ready(1, waiting)
-    waiting = grid_halos(2)
+    grid_ready(1)
     down_0(0)
-    wait(moving)
-    blank(nu3, in3, [(0, H3), (H3 + N3, N3 + 2 * H3)])
-    planes3 = N3 + 2 * H3
-    lo = H3 - 2 - (BOTTOM - 1)
-    weights(
-        lev3, DIFFUSION_NUMBER / 64, lo, planes3 - lo, ANY, nu3, ALL, in3, r["g3"], r["w3"], r["iw3"]
-    )
-    grid_ready(2, waiting)
-    waiting = grid_halos(3)
-    down_0(1)
-    grid_ready(3, waiting)
-    down_0(2)
-
-    x1, x2, x3 = r["x1"], r["x2"], r["x3"]
-    s1, a1, b1 = three("s", 1), three("a", 1), three("b", 1)
-    s2, a2, b2 = three("s", 2), three("a", 2), three("b", 2)
-    s3, a3, b3 = three("s", 3), three("a", 3), three("b", 3)
-    wait(start(halos(x1, N1, H1, r["send_e"].at[2], r["recv_e"].at[2])))
-    blank(x1, in1, [(0, H1), (H1 + N1, N1 + 2 * H1)])
-    scaled(x1, r["w1"], s1, 1, N1 + 2 * H1 - 1)
-    sweep(lev1, 2, N1 + 2 * H1 - 2, ANY, r["g1"], s1, s1, storing(a1))
-
-    def down(level, ms, halo_f, halo_c, g, iw, s, a, x, d):
+    first = to_level_1(0)
+    lo3 = H3 - 2 - (BOTTOM - 1)
+    hi3 = N3 + 2 * H3 - lo3
+    lo2, hi2 = 2 * lo3 - 2, 2 * hi3 + 2
+
+    def down(level, ms, start_f, start_c, g, iw, s, a, x, d):
         made = []
         for m in ms:
-            n = halo_f + 2 * m
-            one = residual(level, n, g, iw, s, a)
-            two = residual(level, n + 1, g, iw, s, a)
-            for c in range(3):
-                made.append((m, c, 0.125 * pair_sum(one[c] + two[c], d)))
-        for m, c, v in made:
-            x[halo_c + m, c] = v
-
-    steps(0, N2, ANY, lambda ms: down(lev1, ms, H1, H2, r["g1"], r["iw1"], s1, a1, x2, 1))
-
-    place2 = lax.rem(row8, 2) * 2 + lax.rem(lane8, 2)
-    pk2, pk3 = r["pk2"], r["pk3"]
-
-    def pack_2(ms):
-        made = []
-        for m in ms:
-            one = x2[H2 + m, 0]
-            for c in (1, 2):
-                one = jnp.where(place2 == c, x2[H2 + m, c], one)
-            made.append((m, one))
-        for m, one in made:
-            pk2[H2 + m] = one
-
-    steps(0, N2, 8, pack_2)
-    wait(start(halos(pk2, N2, H2, r["send_e"].at[3], r["recv_e"].at[3])))
-
-    def unpack_2(ns):
-        made = []
-        for n in ns:
-            packed = jnp.where(in2(n), pk2[n], 0.0)
-            for c in range(3):
-                made.append((n, c, pair_sum(jnp.where(place2 == c, packed, 0.0), 1)))
-        for n, c, v in made:
-            x2[n, c] = v
-
-    steps(0, H2, 6, unpack_2)
-    steps(H2 + N2, N2 + 2 * H2, 6, unpack_2)
-    scaled(x2, r["w2"], s2, 1, N2 + 2 * H2 - 1)
-    sweep(lev2, 2, N2 + 2 * H2 - 2, ANY, r["g2"], s2, s2, storing(a2))
-    steps(0, N3, 4, lambda ms: down(lev2, ms, H2, H3, r["g2"], r["iw2"], s2, a2, x3, 2))
-
-    row_of, lane_of = lax.rem(row8, 4), lax.rem(lane8, 4)
-    made = None
-    for m in range(N3):
-        line = x3[H3 + m, 0]
-        for c in (1, 2):
-            line = jnp.where(lane_of == c, x3[H3 + m, c], line)
-        made = line if made is None else jnp.where(row_of == m, line, made)
-    pk3[REACH] = made
-    wait(
-        start(
-            [
-                exchange(k, pk3.at[REACH], pk3.at[REACH - k], r["send_r3"].at[i], r["recv_r3"].at[i])
-                for i, k in enumerate(hops)
-            ]
+            n = start_f + 2 * m
+            [one] = residual(level, n, g, iw, [s], [a])
+            [two] = residual(level, n + 1, g, iw, [s], [a])
+            made.append((m, 0.125 * pair_sum(one + two, d)))
+        for m, v in made:
+            x[start_c + m] = v
+
+    def to_level_2(c, moving):
+        x, s, a = r[f"x1{c}"], r[f"s1{c}"], r[f"a1{c}"]
+        wait(moving)
+        blank(x, in1, [(0, H1), (H1 + N1, N1 + 2 * H1)])
+        scaled(x, r["w1"], s, 1, N1 + 2 * H1 - 1)
+        sweep(lev1, 2, N1 + 2 * H1 - 2, ANY, r["g1"], [s], [s], storing([a]))
+        steps(
+            0, N2, ANY,
+            lambda ms: down(lev1, ms, H1, H2, r["g1"], r["iw1"], s, a, r[f"x2{c}"], 1),
         )
-    )
-
-    def unpack_3(bs):
-        made = []
-        for b in bs:
-            packed = pk3[b]
-            for m in range(N3):
-                n = N3 * b + m
-                line = jnp.where((row_of == m) & in3(n), packed, 0.0)
-                line = spread_rows(spread_rows(line, 1), 2)
-                for c in range(3):
-                    one = jnp.where(lane_of == c, line, 0.0)
-                    made.append((n, c, spread_lanes(spread_lanes(one, 1), 2)))
-        for n, c, v in made:
-            x3[n, c] = v
-
-    steps(0, REACH, ANY, unpack_3)
-    steps(REACH + 1, 2 * REACH + 1, ANY, unpack_3)
-    scaled(x3, r["w3"], s3, lo, planes3 - lo)
-    src = s3
-    for turn in range(1, BOTTOM):
-        dst = a3 if turn % 2 else b3
-        sweep(
-            lev3, lo + turn, planes3 - lo - turn, ANY, r["g3"], s3, src, storing(dst)
-        )
-        src = dst
-
-    def add(bs, coarse, start_f, start_c):
+        return pack(c, r[f"x2{c}"])
+
+    def add(b, coarse, start_f, start_c):
         def pairs(ms):
             made = []
             for m in ms:
-                for c in range(3):
-                    more = coarse[c][start_c + m]
-                    for twin in (0, 1):
-                        n = start_f + 2 * m + twin
-                        made.append((c, n, bs[c][n] + more))
-            for c, n, v in made:
-                bs[c][n] = v
+                more = coarse[start_c + m]
+                for twin in (0, 1):
+                    n = start_f + 2 * m + twin
+                    made.append((n, b[n] + more))
+            for n, v in made:
+                b[n] = v
 
         return pairs
 
-    steps(0, (N2 + 8) // 2, ANY, add(a2, src, H2 - 4, H3 - 2))
-    sweep(lev2, 3, N2 + 2 * H2 - 3, ANY, r["g2"], s2, a2, storing(b2))
-    sweep(lev2, 4, N2 + 2 * H2 - 4, ANY, r["g2"], s2, b2, storing(a2))
-    steps(0, (N1 + 8) // 2, ANY, add(a1, a2, H1 - 4, H2 - 2))
-    sweep(lev1, 3, N1 + 2 * H1 - 3, ANY, r["g1"], s1, a1, storing(b1))
-    sweep(lev1, 4, N1 + 2 * H1 - 4, ANY, r["g1"], s1, b1, storing(a1))
-
-    wide = N1 + 2
+    def bottom(c, moving):
+        x, s, a, b = (r[f"{kind}2{c}"] for kind in "xsab")
+        unpack(c, x, moving)
+        scaled(x, r["w2"], s, lo2, hi2)
+        sweep(lev2, lo2 + 1, hi2 - 1, ANY, r["g2"], [s], [s], storing([a]))
+        x3, s3, a3, b3 = (r[f"{kind}3{c}"] for kind in "xsab")
+        steps(
+            lo3, hi3, ANY, lambda ms: down(lev2, ms, 0, 0, r["g2"], r["iw2"], s, a, x3, 2)
+        )
+        scaled(x3, r["w3"], s3, lo3, hi3)
+        src = s3
+        for turn in range(1, BOTTOM):
+            dst = a3 if turn % 2 else b3
+            sweep(lev3, lo3 + turn, hi3 - turn, ANY, r["g3"], [s3], [src], storing([dst]))
+            src = dst
+        steps(0, (N2 + 8) // 2, ANY, add(a, src, H2 - 4, H3 - 2))
+        sweep(lev2, H2 - 3, H2 + N2 + 3, ANY, r["g2"], [s], [a], storing([b]))
+        sweep(lev2, H2 - 2, H2 + N2 + 2, ANY, r["g2"], [s], [b], storing([a]))
+        s1, a1, b1 = (r[f"{kind}1{c}"] for kind in "sab")
+        steps(0, (N1 + 8) // 2, ANY, add(a1, a, H1 - 4, H2 - 2))
+        sweep(lev1, 3, N1 + 2 * H1 - 3, ANY, r["g1"], [s1], [a1], storing([b1]))
+        sweep(lev1, 4, N1 + 2 * H1 - 4, ANY, r["g1"], [s1], [b1], storing([a1]))
+
     outs = (o_0, o_1, o_2)
-    for c in range(3):
-        coarse = a1[c][pl.ds(H1 - 1, wide)].reshape(wide * 8, LANES)
+
+    def top(c):
+        wide = N1 + 2
+        coarse = r[f"a1{c}"][pl.ds(H1 - 1, wide)].reshape(wide * 8, LANES)
         for jh in (0, 1):
             half[c, jh] = jnp.dot(
                 coarse, up_m[jh], precision=HIGHEST, preferred_element_type=F32
             ).reshape(wide, 8, LANES)
-
-    for c in range(3):
         s, a, b = r[f"s0{c}"], r[f"a0{c}"], r[f"b0{c}"]
 
-        def refined(ms, c=c, b=b):
+        def refined(ms):
             for i, m in enumerate(ms):
                 for jh in (0, 1):
                     for twin in (0, 1):
@@ -700,34 +699,59 @@
                 put(b, n, v)
 
         steps(0, wide, 9, refined)
-    s0, a0, b0 = three("s", 0), three("a", 0), three("b", 0)
-
-    def to_a0(c, _, n, v):
-        put(a0[c], n, v)
-
-    def to_out(c, _, n, v):
-        outs[c][n - H0] = v
-
-    for c in range(3):
         sweep(
-            fine, 3, N0 + 2 * H0 - 3, 17, r["g0"], [s0[c]], [b0[c]],
-            functools.partial(to_a0, c), BODY,
+            fine, 3, N0 + 2 * H0 - 3, 17, r["g0"], [s], [b], lambda _, n, v: put(a, n, v), BODY
         )
-        sweep(
-            fine, 4, N0 + 2 * H0 - 4, 16, r["g0"], [s0[c]], [a0[c]],
-            functools.partial(to_out, c), BODY,
-        )
+
+        def to_out(_, n, v):
+            outs[c][n - H0] = v
+
+        sweep(fine, 4, N0 + 2 * H0 - 4, 16, r["g0"], [s], [a], to_out, BODY)
+
+    first = to_level_2(0, first)
+    grid_ready(2)
+    down_0(1)
+    second = to_level_1(1)
+    unpack(3, nu2, moving)
+    steps(lo3 - 1, hi3 + 1, 12, nu_down(nu2, nu3, 0, 0, 2))
+    weights(
+        lev2, DIFFUSION_NUMBER / 16, lo2, hi2, 24, nu2, ALL, in2, r["g2"], r["w2"], r["iw2"]
+    )
+    weights(
+        lev3, DIFFUSION_NUMBER / 64, lo3, hi3, ANY, nu3, ALL, in3, r["g3"], r["w3"], r["iw3"]
+    )
+    second = to_level_2(1, second)
+    grid_ready(3)
+    down_0(2)
+    third = to_level_1(2)
+    bottom(0, first)
+    bottom(1, second)
+    third = to_level_2(2, third)
+    top(0)
+    top(1)
+    bottom(2, third)
+    top(2)
 
     for f in range(4):
-        most = stages[f].at[pl.ds(0, (n_dev - 1) * rows)]
+        most = mids[f].at[pl.ds(0, n_dev - 1)]
         pltpu.make_async_copy(most, most, r["send_1"].at[f]).wait()
-        most = asms[f].at[pl.ds(0, n_dev - 1)]
-        pltpu.make_async_copy(most, most, r["send_2"].at[f]).wait()
+
+        @pl.when((dev > 0) & (dev < n_dev - 1))
+        def _():
+            most = asms[f].at[pl.ds(0, n_dev - 1)]
+            pltpu.make_async_copy(most, most, r["send_2"].at[f]).wait()
+
+        @pl.when((dev == 0) | (dev == n_dev - 1))
+        def _():
+            most = stages[f].reshape(SIDE * SIDE // 8, 8, LANES).at[pl.ds(0, 128)]
+            pltpu.make_async_copy(most, most, r["send_2"].at[f]).wait()
+            rest = stages[f].reshape(SIDE * SIDE // 8, 8, LANES).at[pl.ds(0, 23)]
+            pltpu.make_async_copy(rest, rest, r["send_2"].at[f]).wait()
 
 
 def whole(n_dev, source, velocity_old, viscosity_old):
     vmem = pl.BlockSpec(memory_space=pltpu.VMEM)
-    anywhere = pl.BlockSpec(memory_space=pl.ANY)
+    anywhere = pl.BlockSpec(memory_space=pltpu.HBM)
     named = names_of_scratch(n_dev)
     return pl.pallas_call(
         functools.partial(whole_kernel, tuple(named)),

time: 103 us -> 97.8 us (0.950)
  Pallas kernels: 99.8 us -> 94.5 us
    pallas_call x1, Pallas kernels: 97.8 us -> 92.4 us  [whole(): pl.pallas_call(functools.partial(whole_kernel, tuple(named)), out_shape=[...]
where the time goes in v4:
time: 97.8 us; the launch traced here: 97.6 us
  Pallas kernels  94.5 us (97%)
  local copies, waits for them, and re-layouts  3.13 us (3%)
    pallas_call x1, Pallas kernels, whole(): pl.pallas_call(functools.partial(whole_kernel, tuple(named)), out_shape=[...  92.4 us
    unnamed x6, local copies, waits for them, and re-layouts  3.13 us
    pallas_call x1, Pallas kernels, to_blocks(): pl.pallas_call(blocks_kernel, out_shape=jax.ShapeDtypeStruct((4, 3, SIDE,...  2.07 us

profile of v4, /device:TPU:0, one launch (start us, length us, event | category | flops | bytes accessed | tf_op | source)
XLA Modules:
  0.0 97.6 jit_solution(15294207499642604524)
XLA Ops:
  0.0 0.0 copy-start
  0.0 1.4 %copy-done = f32[4,3,32,1024]{3,2,1,0:T(8,128)S(1)} copy-done((f32[4,3,32,1024]{3,2,1,0:T(8,128)S(1)}, f32[4,3,32,1024]{3,2,1,0:T(8,128)}, u32[]{:S(2)}) %copy-start) | copy-done | bytes 1572888
  1.4 0.0 copy-start.1
  1.4 1.0 %copy-done.1 = f32[4,32,1024]{2,1,0:T(8,128)S(1)} copy-done((f32[4,32,1024]{2,1,0:T(8,128)S(1)}, f32[4,32,1024]{2,1,0:T(8,128)}, u32[]{:S(2)}) %copy-start.1) | copy-done | bytes 524312
  2.5 0.0 copy-start.2
  2.5 0.7 copy-done.2
  3.1 92.4 %whole.1 = (f32[32,32,128]{2,1,0:T(8,128)S(1)}, f32[32,32,128]{2,1,0:T(8,128)S(1)}, f32[32,32,128]{2,1,0:T(8,128)S(1)}) custom-call(s32[512]{0:T(512)S(1)} %copy-done.2, f32[4,3,32,1024]{3,2,1,0:T(8,128)S(1)} %copy-done, f32[4,32,1024]{2,1,0:T(8,128)S(1)} %copy-done.1), custom_call_target="tpu_custom_call" | custom-call | tf_op jit(solution)/shard_map/whole/pallas_call | solution.py:756
  95.5 2.1 %to_blocks.1 = f32[4,3,32,1024]{3,2,1,0:T(8,128)} custom-call(f32[1024,128]{1,0:T(8,128)S(1)} %bitcast.3, f32[1024,128]{1,0:T(8,128)S(1)} %bitcast.4, f32[1024,128]{1,0:T(8,128)S(1)} %bitcast.5), custom_call_target="tpu_custom_call" | custom-call | tf_op jit(solution)/shard_map/to_blocks/pallas_call | solution.py:780
Async XLA Ops:
  0.0 1.4 %copy-start = (f32[4,3,32,1024]{3,2,1,0:T(8,128)S(1)}, f32[4,3,32,1024]{3,2,1,0:T(8,128)}, u32[]{:S(2)}) copy-start(f32[4,3,32,1024]{3,2,1,0:T(8,128)} %vel_hbm.1) | copy-start | bytes 4718596
  1.4 1.0 %copy-start.1 = (f32[4,32,1024]{2,1,0:T(8,128)S(1)}, f32[4,32,1024]{2,1,0:T(8,128)}, u32[]{:S(2)}) copy-start(f32[4,32,1024]{2,1,0:T(8,128)} %vis_hbm.1) | copy-start | bytes 1572868
  2.5 0.7 copy-start.2

commit v5 on v4

--- a/solution.py
+++ b/solution.py
@@ -308,7 +308,7 @@
         tiles = stages[f].reshape(STRIDE_TILES, 4, 4, 8, LANES)
 
         def send(t, carry):
-            to = lax.rem(dev + t, n_dev)
+            to = lax.rem(phase + t // 4, 4) * 4 + lax.rem(rg + lax.rem(t, 4), 4)
             pltpu.make_async_remote_copy(
                 src_ref=tiles.at[:, to // 4, lax.rem(to, 4)],
                 dst_ref=mids[f].at[dev],
@@ -377,7 +377,7 @@
                 copy(d, 0, far + 1, (grp, d))
 
         def send(t, carry):
-            to_device(remote, lax.rem(dev + t, n_dev))
+            to_device(remote, lax.rem(phase + t // 4, 4) * 4 + lax.rem(rg + lax.rem(t, 4), 4))
             return carry
 
         lax.fori_loop(1, n_dev, send, 0)

time: 97.8 us -> 98.7 us (level)
  no operation moved by 1% of the time
where the time goes in v5:
time: 98.7 us; the launch traced here: 98.5 us
  Pallas kernels  95.4 us (97%)
  local copies, waits for them, and re-layouts  3.13 us (3%)
    pallas_call x1, Pallas kernels, whole(): pl.pallas_call(functools.partial(whole_kernel, tuple(named)), out_shape=[...  93.3 us
    unnamed x6, local copies, waits for them, and re-layouts  3.13 us
    pallas_call x1, Pallas kernels, to_blocks(): pl.pallas_call(blocks_kernel, out_shape=jax.ShapeDtypeStruct((4, 3, SIDE,...  2.07 us

profile of v5, /device:TPU:0, one launch (start us, length us, event | category | flops | bytes accessed | tf_op | source)
XLA Modules:
  0.0 98.5 jit_solution(4648909396334628511)
XLA Ops:
  0.0 0.0 copy-start
  0.0 1.4 %copy-done = f32[4,3,32,1024]{3,2,1,0:T(8,128)S(1)} copy-done((f32[4,3,32,1024]{3,2,1,0:T(8,128)S(1)}, f32[4,3,32,1024]{3,2,1,0:T(8,128)}, u32[]{:S(2)}) %copy-start) | copy-done | bytes 1572888
  1.4 0.0 copy-start.1
  1.4 1.0 %copy-done.1 = f32[4,32,1024]{2,1,0:T(8,128)S(1)} copy-done((f32[4,32,1024]{2,1,0:T(8,128)S(1)}, f32[4,32,1024]{2,1,0:T(8,128)}, u32[]{:S(2)}) %copy-start.1) | copy-done | bytes 524312
  2.5 0.0 copy-start.2
  2.5 0.7 copy-done.2
  3.1 93.3 %whole.1 = (f32[32,32,128]{2,1,0:T(8,128)S(1)}, f32[32,32,128]{2,1,0:T(8,128)S(1)}, f32[32,32,128]{2,1,0:T(8,128)S(1)}) custom-call(s32[512]{0:T(512)S(1)} %copy-done.2, f32[4,3,32,1024]{3,2,1,0:T(8,128)S(1)} %copy-done, f32[4,32,1024]{2,1,0:T(8,128)S(1)} %copy-done.1), custom_call_target="tpu_custom_call" | custom-call | tf_op jit(solution)/shard_map/whole/pallas_call | solution.py:756
  96.5 2.1 %to_blocks.1 = f32[4,3,32,1024]{3,2,1,0:T(8,128)} custom-call(f32[1024,128]{1,0:T(8,128)S(1)} %bitcast.3, f32[1024,128]{1,0:T(8,128)S(1)} %bitcast.4, f32[1024,128]{1,0:T(8,128)S(1)} %bitcast.5), custom_call_target="tpu_custom_call" | custom-call | tf_op jit(solution)/shard_map/to_blocks/pallas_call | solution.py:780
Async XLA Ops:
  0.0 1.4 %copy-start = (f32[4,3,32,1024]{3,2,1,0:T(8,128)S(1)}, f32[4,3,32,1024]{3,2,1,0:T(8,128)}, u32[]{:S(2)}) copy-start(f32[4,3,32,1024]{3,2,1,0:T(8,128)} %vel_hbm.1) | copy-start | bytes 4718596
  1.4 1.0 %copy-start.1 = (f32[4,32,1024]{2,1,0:T(8,128)S(1)}, f32[4,32,1024]{2,1,0:T(8,128)}, u32[]{:S(2)}) copy-start(f32[4,32,1024]{2,1,0:T(8,128)} %vis_hbm.1) | copy-start | bytes 1572868
  2.5 0.7 copy-start.2

commit v6 on v4

--- a/solution.py
+++ b/solution.py
@@ -292,8 +292,14 @@
 
         lax.fori_loop(0, n_dev, onward, 0)
 
+    crossing = 0
     for k in hops:
-        pl.semaphore_signal(barrier, inc=1, device_id=stream_device(k), device_id_type=MESH)
+        outside = (dev + k < 0) | (dev + k >= n_dev)
+        crossing = crossing + jnp.where(outside, 1, 0)
+
+        @pl.when(outside)
+        def _(k=k):
+            pl.semaphore_signal(barrier, inc=1, device_id=stream_device(k), device_id_type=MESH)
 
     def transpose_field(f):
         for t in range(8):
@@ -584,7 +590,7 @@
     for f in range(4):
         staged(f)
     ends = jnp.where((dev == 0) | (dev == n_dev - 1), n_dev, 0)
-    pl.semaphore_wait(barrier, n_dev - 1 + len(hops) + 2 + ends)
+    pl.semaphore_wait(barrier, n_dev - 1 + crossing + 2 + ends)
     spread(0)
     spread(1)
     collect(0)

time: 97.8 us -> 98.1 us (level)
  no operation moved by 1% of the time
where the time goes in v6:
time: 98.1 us; the launch traced here: 97.9 us
  Pallas kernels  94.8 us (97%)
  local copies, waits for them, and re-layouts  3.13 us (3%)
    pallas_call x1, Pallas kernels, whole(): pl.pallas_call(functools.partial(whole_kernel, tuple(named)), out_shape=[...  92.7 us
    unnamed x6, local copies, waits for them, and re-layouts  3.13 us
    pallas_call x1, Pallas kernels, to_blocks(): pl.pallas_call(blocks_kernel, out_shape=jax.ShapeDtypeStruct((4, 3, SIDE,...  2.07 us

profile of v6, /device:TPU:0, one launch (start us, length us, event | category | flops | bytes accessed | tf_op | source)
XLA Modules:
  0.0 97.9 jit_solution(15211395492977332313)
XLA Ops:
  0.0 0.0 copy-start
  0.0 1.4 %copy-done = f32[4,3,32,1024]{3,2,1,0:T(8,128)S(1)} copy-done((f32[4,3,32,1024]{3,2,1,0:T(8,128)S(1)}, f32[4,3,32,1024]{3,2,1,0:T(8,128)}, u32[]{:S(2)}) %copy-start) | copy-done | bytes 1572888
  1.4 0.0 copy-start.1
  1.4 1.0 %copy-done.1 = f32[4,32,1024]{2,1,0:T(8,128)S(1)} copy-done((f32[4,32,1024]{2,1,0:T(8,128)S(1)}, f32[4,32,1024]{2,1,0:T(8,128)}, u32[]{:S(2)}) %copy-start.1) | copy-done | bytes 524312
  2.5 0.0 copy-start.2
  2.5 0.7 copy-done.2
  3.1 92.7 %whole.1 = (f32[32,32,128]{2,1,0:T(8,128)S(1)}, f32[32,32,128]{2,1,0:T(8,128)S(1)}, f32[32,32,128]{2,1,0:T(8,128)S(1)}) custom-call(s32[512]{0:T(512)S(1)} %copy-done.2, f32[4,3,32,1024]{3,2,1,0:T(8,128)S(1)} %copy-done, f32[4,32,1024]{2,1,0:T(8,128)S(1)} %copy-done.1), custom_call_target="tpu_custom_call" | custom-call | tf_op jit(solution)/shard_map/whole/pallas_call | solution.py:762
  95.9 2.1 %to_blocks.1 = f32[4,3,32,1024]{3,2,1,0:T(8,128)} custom-call(f32[1024,128]{1,0:T(8,128)S(1)} %bitcast.3, f32[1024,128]{1,0:T(8,128)S(1)} %bitcast.4, f32[1024,128]{1,0:T(8,128)S(1)} %bitcast.5), custom_call_target="tpu_custom_call" | custom-call | tf_op jit(solution)/shard_map/to_blocks/pallas_call | solution.py:786
Async XLA Ops:
  0.0 1.4 %copy-start = (f32[4,3,32,1024]{3,2,1,0:T(8,128)S(1)}, f32[4,3,32,1024]{3,2,1,0:T(8,128)}, u32[]{:S(2)}) copy-start(f32[4,3,32,1024]{3,2,1,0:T(8,128)} %vel_hbm.1) | copy-start | bytes 4718596
  1.4 1.0 %copy-start.1 = (f32[4,32,1024]{2,1,0:T(8,128)S(1)}, f32[4,32,1024]{2,1,0:T(8,128)}, u32[]{:S(2)}) copy-start(f32[4,32,1024]{2,1,0:T(8,128)} %vis_hbm.1) | copy-start | bytes 1572868
  2.5 0.7 copy-start.2
